TPU v7x, 128 devices: a whole 4x4x4 slice. The times are simulated.
128 devices in a mesh: fsdp: 32 (over y, z, x_hi), tenant: 4 (over x_lo, core).
Axes of the slice: x: 4 (x_hi: 2, x_lo: 2; x = x_hi * 2 + x_lo), y: 4, z: 4, core: 2. Of those that a mesh axis runs over, the one named last changes fastest.
Arguments:
- tokens: bfloat16 [32768, 16384], P(('fsdp', 'tenant'))
- cotangent: bfloat16 [32768, 16384], P(('fsdp', 'tenant')), may hold values from -6 to 6
- w_query: bfloat16 [16384, 256], P('fsdp'), may hold values from -0.046875 to 0.046875
- w_key: bfloat16 [16384, 128], P('fsdp'), may hold values from -0.046875 to 0.046875
- w_value: bfloat16 [16384, 128], P('fsdp'), may hold values from -0.046875 to 0.046875
- w_output: bfloat16 [256, 16384], P(None, 'fsdp'), may hold values from -0.375 to 0.375
- adapter_down: bfloat16 [16384, 8, 2, 16], P('fsdp', 'tenant'), may hold values from -0.046875 to 0.046875
- adapter_up: bfloat16 [8, 16, 384], P('tenant'), may hold values from -1.5 to 1.5
- tenant_slot: int32 [128], P(('fsdp', 'tenant')), may hold values from 0 to 1
- lengths: int32 [128], P(('fsdp', 'tenant')), may hold values from 1 to 256, as said below
Outputs:
- output: bfloat16 [32768, 16384], P(('fsdp', 'tenant'))
- grad_down: float32 [16384, 8, 2, 16], P('fsdp', 'tenant')
- grad_up: float32 [8, 16, 384], P('tenant')
Inputs may be any that keep to these rules, and one draw needn't show every extreme that they name: `lengths`: sample 0 has all 256 tokens real; the others at least one.
All inputs are finite; a program needn't handle non-finite values.
Results may differ from a plain program's by a relative error of at most 0.0075.
The roundings to bfloat16 on the way count: a program that leaves them out, or rounds other values in their place, can miss the bound.
Values may be sent and summed in bfloat16 or wider, within the bound.
No kernel may reach another device: no remote copies, remote signals or barrier semaphores. Data moves between devices by JAX's collectives and lax.ppermute only.
A program may use at most 192 MiB of HBM per device.

v0:
```python
import jax
import jax.numpy as jnp
from jax import lax
from jax.sharding import PartitionSpec as P

ADAPTER_SCALE = 2.0


def body(
    tokens,
    cotangent,
    w_query,
    w_key,
    w_value,
    w_output,
    adapter_down,
    adapter_up,
    tenant_slot,
    lengths,
):
    seq_len, width = tokens.shape
    q_width = w_query.shape[1]
    head = w_key.shape[1]
    heads = q_width // head
    shard_rows, ten_local, _, rank = adapter_down.shape
    low_cols = ten_local * 2 * rank
    slot = tenant_slot[0]
    length = lengths[0]
    inv_root = 1.0 / jnp.sqrt(jnp.float32(head))
    columns = tokens
    updated_query = jnp.dot(
        columns,
        lax.all_gather(w_query, "fsdp", axis=0, tiled=True),
        preferred_element_type=jnp.float32,
    )
    new_k = jnp.dot(
        columns,
        lax.all_gather(w_key, "fsdp", axis=0, tiled=True),
        preferred_element_type=jnp.float32,
    )
    updated_value = jnp.dot(
        columns,
        lax.all_gather(w_value, "fsdp", axis=0, tiled=True),
        preferred_element_type=jnp.float32,
    )
    piece = lax.all_gather(adapter_down, "fsdp", axis=0, tiled=True)
    count = piece.shape[0]
    columns = tokens
    new_low = jnp.dot(columns, piece.reshape(count, low_cols), preferred_element_type=jnp.float32)
    low_rank_rows = lax.dynamic_index_in_dim(
        new_low.reshape(seq_len, ten_local, 2, rank), slot, 1, keepdims=False
    ).astype(jnp.bfloat16)
    up_sel = lax.dynamic_index_in_dim(adapter_up, slot, 0, keepdims=False)
    query_up_weight = up_sel[:, :q_width]
    value_up_weight = up_sel[:, q_width:]
    query_rows = (
        updated_query
        + ADAPTER_SCALE
        * jnp.dot(low_rank_rows[:, 0], query_up_weight, preferred_element_type=jnp.float32)
    ).astype(jnp.bfloat16)
    key = new_k.astype(jnp.bfloat16)
    value_rows = (
        updated_value
        + ADAPTER_SCALE
        * jnp.dot(low_rank_rows[:, 1], value_up_weight, preferred_element_type=jnp.float32)
    ).astype(jnp.bfloat16)
    positions = jnp.arange(seq_len, dtype=jnp.int32)
    valid = positions < length
    mask = (positions[None, :] <= positions[:, None]) & valid[None, :]
    keep = valid.astype(jnp.float32)[:, None]
    probs_list = []
    ctx_list = []
    for head_idx in range(heads):
        q_head = query_rows[:, head_idx * head : (head_idx + 1) * head]
        scores = (
            lax.dot_general(
                q_head, key, (((1,), (1,)), ((), ())), preferred_element_type=jnp.float32
            )
            * inv_root
        )
        scores = jnp.where(mask, scores, jnp.float32(-1e30))
        top = jnp.max(scores, axis=1, keepdims=True)
        expo = jnp.where(mask, jnp.exp(scores - top), jnp.float32(0.0))
        probs = expo / jnp.sum(expo, axis=1, keepdims=True)
        probs_list.append(probs)
        ctx_list.append(
            jnp.dot(probs.astype(jnp.bfloat16), value_rows, preferred_element_type=jnp.float32)
        )
    context = (jnp.concatenate(ctx_list, axis=1) * keep).astype(jnp.bfloat16)
    output = jnp.dot(
        context,
        lax.all_gather(w_output, "fsdp", axis=1, tiled=True),
        preferred_element_type=jnp.float32,
    ).astype(jnp.bfloat16)
    columns = cotangent
    d_context = lax.dot_general(
        columns,
        lax.all_gather(w_output, "fsdp", axis=1, tiled=True),
        (((1,), (1,)), ((), ())),
        preferred_element_type=jnp.float32,
    )
    d_context = (d_context * keep).astype(jnp.bfloat16)
    value_acc = jnp.zeros((seq_len, head), jnp.float32)
    dq_list = []
    for head_idx in range(heads):
        probs = probs_list[head_idx]
        probs_b = probs.astype(jnp.bfloat16)
        d_ctx_head = d_context[:, head_idx * head : (head_idx + 1) * head]
        d_probs = lax.dot_general(
            d_ctx_head, value_rows, (((1,), (1,)), ((), ())), preferred_element_type=jnp.float32
        )
        value_acc = value_acc + lax.dot_general(
            probs_b, d_ctx_head, (((0,), (0,)), ((), ())), preferred_element_type=jnp.float32
        )
        delta = jnp.sum(probs * d_probs, axis=1, keepdims=True)
        d_scores = (probs * (d_probs - delta)).astype(jnp.bfloat16)
        dq_list.append(jnp.dot(d_scores, key, preferred_element_type=jnp.float32) * inv_root)
    value_gradient = value_acc.astype(jnp.bfloat16)
    query_gradient = jnp.concatenate(dq_list, axis=1).astype(jnp.bfloat16)
    selector = (jnp.arange(ten_local, dtype=jnp.int32) == slot).astype(jnp.float32)
    query_summand = lax.dot_general(
        low_rank_rows[:, 0],
        query_gradient,
        (((0,), (0,)), ((), ())),
        preferred_element_type=jnp.float32,
    )
    value_summand = lax.dot_general(
        low_rank_rows[:, 1],
        value_gradient,
        (((0,), (0,)), ((), ())),
        preferred_element_type=jnp.float32,
    )
    up_summand = ADAPTER_SCALE * jnp.concatenate([query_summand, value_summand], axis=1)
    up_summand = selector[:, None, None] * up_summand[None]
    query_middle = ADAPTER_SCALE * lax.dot_general(
        query_gradient,
        query_up_weight,
        (((1,), (1,)), ((), ())),
        preferred_element_type=jnp.float32,
    )
    value_middle = ADAPTER_SCALE * lax.dot_general(
        value_gradient,
        value_up_weight,
        (((1,), (1,)), ((), ())),
        preferred_element_type=jnp.float32,
    )
    mid = jnp.stack([query_middle, value_middle], axis=1).astype(jnp.bfloat16)
    mid_full = (selector.astype(jnp.bfloat16)[None, :, None, None] * mid[:, None]).reshape(
        seq_len, low_cols
    )
    columns = tokens
    term = lax.dot_general(
        columns, mid_full, (((0,), (0,)), ((), ())), preferred_element_type=jnp.float32
    )
    grad_down = lax.psum_scatter(
        term.reshape(shard_rows * lax.axis_size("fsdp"), ten_local, 2, rank),
        "fsdp",
        scatter_dimension=0,
        tiled=True,
    )
    grad_up = lax.psum(up_summand, "fsdp")
    return (output, grad_down, grad_up)


def solution(mesh):
    placed = (
        P(("fsdp", "tenant"), None),
        P(("fsdp", "tenant"), None),
        P("fsdp", None),
        P("fsdp", None),
        P("fsdp", None),
        P(None, "fsdp"),
        P("fsdp", "tenant", None, None),
        P("tenant", None, None),
        P(("fsdp", "tenant")),
        P(("fsdp", "tenant")),
    )
    return jax.shard_map(
        body,
        mesh=mesh,
        in_specs=placed,
        out_specs=(
            P(("fsdp", "tenant"), None),
            P("fsdp", "tenant", None, None),
            P("tenant", None, None),
        ),
        check_vma=False,
    )
```

profile of v0, /device:TPU:2, one launch (start us, length us, event | category | flops | bytes accessed | tf_op | source)
XLA Modules:
  0.0 692.5 jit_solution(5298667718356597786)
XLA Ops:
  7.2 0.0 copy-start
  7.2 0.0 all-gather.8.cloned.1.call-start
  7.2 0.7 all-gather.8.cloned.1.call-update
  7.9 0.0 all-gather.12.cloned.1.call-start
  8.0 0.7 all-gather.12.cloned.1.call-update
  8.7 0.0 all-gather.10.cloned.1.call-start
  8.7 0.7 all-gather.10.cloned.1.call-update
  9.4 0.0 all-gather.6.cloned.1.call-start
  9.4 0.5 all-gather.6.cloned.1.call-update
  10.0 0.0 all-gather.14.cloned.1.call-start
  10.0 0.5 all-gather.14.cloned.1.call-update
  10.6 0.0 reduce-scatter.2.cloned.1.call-start
  11.9 0.1 mul.107
  12.0 0.1 mul.108
  12.1 71.5 %all-gather.8.cloned.1.call-done = bf16[16384,2,2,16]{0,3,2,1:T(8,128)(2,1)} async-done(((bf16[512,2,2,16]{0,3,2,1:T(8,128)(2,1)}), bf16[16384,2,2,16]{0,3,2,1:T(8,128)(2,1)}) %all-gather.8.cloned.1.call-update) | async-done | bytes 2097168 | tf_op jit(solution)/shard_map/all_gather | solution.py:46
  83.6 6.6 fusion
  90.3 75.9 %all-gather.12.cloned.1.call-done = bf16[16384,128]{1,0:T(8,128)(2,1)} async-done(((bf16[512,128]{1,0:T(8,128)(2,1)}), bf16[16384,128]{1,0:T(8,128)(2,1)}) %all-gather.12.cloned.1.call-update) | async-done | bytes 4194320 | tf_op jit(solution)/shard_map/all_gather | solution.py:43
  166.2 7.1 %fusion.63 = f32[256,128]{1,0:T(8,128)S(1)} fusion(bf16[256,16384]{1,0:T(8,128)(2,1)} %param.10, bf16[16384,128]{1,0:T(8,128)(2,1)} %all-gather.12.cloned.1.call-done), kind=kOutput, calls=%fused_computation.87 | convolution fusion | flops 1073741824 | bytes 12713984 | tf_op jit(solution)/shard_map/dot_general | solution.py:41
  173.2 0.2 fusion.9
  173.5 75.2 %all-gather.10.cloned.1.call-done = bf16[16384,128]{1,0:T(8,128)(2,1)} async-done(((bf16[512,128]{1,0:T(8,128)(2,1)}), bf16[16384,128]{1,0:T(8,128)(2,1)}) %all-gather.10.cloned.1.call-update) | async-done | bytes 4194320 | tf_op jit(solution)/shard_map/all_gather | solution.py:38
  248.6 6.9 convolution_convert_fusion.1
  255.5 98.8 %all-gather.6.cloned.1.call-done = bf16[16384,256]{1,0:T(8,128)(2,1)} async-done(((bf16[512,256]{1,0:T(8,128)(2,1)}), bf16[16384,256]{1,0:T(8,128)(2,1)}) %all-gather.6.cloned.1.call-update) | async-done | bytes 8388624 | tf_op jit(solution)/shard_map/all_gather | solution.py:33
  354.3 8.1 %fusion.62 = f32[256,256]{1,0:T(8,128)S(1)} fusion(bf16[256,16384]{1,0:T(8,128)(2,1)} %param.10, bf16[16384,256]{1,0:T(8,128)(2,1)} %all-gather.6.cloned.1.call-done), kind=kOutput, calls=%fused_computation.86 | convolution fusion | flops 2147483648 | bytes 17039360 | tf_op jit(solution)/shard_map/dot_general | solution.py:31
  362.4 0.2 fusion.6
  362.6 0.2 fusion.61
  362.8 0.2 fusion.60
  363.1 107.0 %all-gather.14.cloned.1.call-done = bf16[256,16384]{1,0:T(8,128)(2,1)} async-done(((bf16[256,512]{1,0:T(8,128)(2,1)}), bf16[256,16384]{1,0:T(8,128)(2,1)}) %all-gather.14.cloned.1.call-update) | async-done | bytes 8388624 | tf_op jit(solution)/shard_map/all_gather | solution.py:92
  470.1 8.1 %fusion.7 = bf16[256,256]{1,0:T(8,128)(2,1)S(1)} fusion(bf16[256,16384]{1,0:T(8,128)(2,1)} %param.11, bf16[256,16384]{1,0:T(8,128)(2,1)} %all-gather.14.cloned.1.call-done, f32[256]{0:T(256)S(1)} %fusion.53), kind=kOutput, calls=%fused_computation.12 | convolution fusion | flops 2147614720 | bytes 16909312 | tf_op jit(solution)/shard_map/dot_general | solution.py:96
  478.2 0.2 fusion.38
  478.4 0.1 fusion.20
  478.6 0.2 fusion.33
  478.8 0.2 multiply_reduce_fusion.1
  479.0 0.3 fusion.11
  479.3 0.4 fusion.12
  479.7 0.1 fusion.16
  479.9 0.3 fusion.10
  480.2 0.1 fusion.15
  480.3 0.1 bitcast_multiply_fusion
  480.4 6.9 %fusion.64 = f32[64,16384]{1,0:T(8,128)} fusion(bf16[256,64]{0,1:T(8,128)(2,1)S(1)} %bitcast_multiply_fusion, bf16[256,16384]{1,0:T(8,128)(2,1)} %param.10), kind=kOutput, calls=%fused_computation.88 | convolution fusion | flops 536870912 | bytes 12615680 | tf_op jit(solution)/shard_map/dot_general | solution.py:152
  487.3 0.0 reduce-scatter.2.cloned.1.call-update
  487.4 0.1 fusion.27
  487.5 0.2 fusion.44
  487.7 0.1 broadcast_multiply_fusion
  487.8 183.1 %psum.7 = f32[2,16,384]{2,1,0:T(8,128)} all-reduce(f32[2,16,384]{2,1,0:T(8,128)S(1)} %broadcast_multiply_fusion), channel_id=1, replica_groups=mesh['fsdp'=32,'tenant'=4] {'fsdp'}, use_global_device_ids=true, to_apply=%region_7.8 | all-reduce | flops 12288 | bytes 98304 | tf_op jit(solution)/shard_map/psum | solution.py:161
  670.9 0.3 fusion.35
  671.2 0.3 fusion.31
  671.5 9.2 %convolution_convert_fusion = bf16[256,16384]{1,0:T(8,128)(2,1)} fusion(bf16[256,16384]{1,0:T(8,128)(2,1)} %all-gather.14.cloned.1.call-done, f32[256,128]{1,0:T(8,128)S(1)} %fusion.31, f32[256,128]{1,0:T(8,128)S(1)} %fusion.35, f32[256]{0:T(256)S(1)} %fusion.53), kind=kOutput, calls=%fused_computation | convolution fusion | flops 2151874560 | bytes 17040384 | tf_op jit(solution)/shard_map/dot_general | solution.py:90
  680.7 4.9 reduce-scatter.2.cloned.1.call-done
  (9 shorter events, 0.1 us)
Async XLA Ops:
  7.2 4.9 copy-start
  7.2 76.5 %all-gather.8.cloned.1.call-start = ((), (), s32[]{:S(2)}) async-start(), calls=%async_computation.2 | async-start | bytes 2162688 | tf_op jit(solution)/shard_map/all_gather | solution.py:46
  7.9 158.2 %all-gather.12.cloned.1.call-start = ((), (), s32[]{:S(2)}) async-start(), calls=%async_computation.4 | async-start | bytes 4325376 | tf_op jit(solution)/shard_map/all_gather | solution.py:43
  8.7 239.9 %all-gather.10.cloned.1.call-start = ((), (), s32[]{:S(2)}) async-start(), calls=%async_computation.3 | async-start | bytes 4325376 | tf_op jit(solution)/shard_map/all_gather | solution.py:38
  9.4 344.9 %all-gather.6.cloned.1.call-start = ((), (), s32[]{:S(2)}) async-start(), calls=%async_computation.1 | async-start | bytes 8650752 | tf_op jit(solution)/shard_map/all_gather | solution.py:33
  10.0 460.1 %all-gather.14.cloned.1.call-start = ((), (), s32[]{:S(2)}) async-start(), calls=%async_computation.5 | async-start | bytes 8650752 | tf_op jit(solution)/shard_map/all_gather | solution.py:92
  10.6 675.1 %reduce-scatter.2.cloned.1.call-start = ((), (), s32[]{:S(2)}) async-start(), calls=%async_computation.6 | async-start | bytes 4325376 | tf_op jit(solution)/shard_map/reduce_scatter | solution.py:155
Sparse Core Ops, SparseCore 0:
  10.8 72.8 all-gather.7
  86.7 79.4 all-gather.11
  169.2 79.3 all-gather.9
  251.6 102.6 all-gather.5
  356.9 113.1 all-gather.13
  487.5 198.1 reduce-scatter.1
where the time goes:
time: 693 us; the launch traced here: 692 us
  waiting for transfers between devices  436 us (63%)
  blocking collectives  183 us (26%)
  matrix products  56.7 us (8%)
  between operations  15.5 us (2%)
    psum x1, blocking collectives, body(): grad_up = lax.psum(up_summand, 'fsdp')  183 us
    all_gather x1, waiting for transfers between devices, body(): lax.all_gather(w_output, 'fsdp', axis=1, tiled=True)  107 us
    all_gather x1, waiting for transfers between devices, body(): lax.all_gather(w_query, 'fsdp', axis=0, tiled=True)  98.8 us
    all_gather x1, waiting for transfers between devices, body(): lax.all_gather(w_value, 'fsdp', axis=0, tiled=True)  75.9 us
    all_gather x1, waiting for transfers between devices, body(): lax.all_gather(w_key, 'fsdp', axis=0, tiled=True)  75.2 us
    all_gather x1, waiting for transfers between devices, body(): piece = lax.all_gather(adapter_down, 'fsdp', axis=0, tiled=True)  71.5 us
  transfers between devices with their start and end apart: 6, of which 6 were waited for; matrix products, arithmetic and copies ran while one was open for 6% of the time, Pallas kernels for 0%

commit v1 on v0

v1 whole, which is shorter than its diff:
```python
import jax
import jax.numpy as jnp
from jax import lax
from jax.experimental import pallas as pl
from jax.experimental.pallas import tpu as pltpu
from jax.sharding import PartitionSpec as P

ADAPTER_SCALE = 2.0
VMEM = 48 * 1024 * 1024
NT = (((1,), (1,)), ((), ()))
TN = (((0,), (0,)), ((), ()))
F32 = jnp.float32
BF16 = jnp.bfloat16


def dot(a, b, dims=(((1,), (0,)), ((), ()))):
    return lax.dot_general(a, b, dims, preferred_element_type=F32)


def params(**kw):
    return pltpu.CompilerParams(vmem_limit_bytes=VMEM, **kw)


def project_kernel(where, tok, cot, frozen, down_a, down_b, qkv, low, dctx):
    @pl.when(pl.program_id(0) == 0)
    def _():
        qkv[...] = jnp.zeros_like(qkv)
        low[...] = jnp.zeros_like(low)
        dctx[...] = jnp.zeros_like(dctx)

    q_cols = qkv.shape[1]
    qkv[...] += dot(tok[...], frozen[:, :q_cols])
    dctx[...] += dot(cot[...], frozen[:, q_cols:])
    shards, half = down_a.shape[0], down_a.shape[3]
    for i in range(shards):
        for h, down in enumerate((down_a, down_b)):
            at = (2 * i + h) * half
            low[...] += dot(tok[:, at : at + half], down[i, 0], NT)


def project(tokens, cotangent, gathered, tenant, slot, q_cols, d_cols, tenants):
    seq, width = tokens.shape
    block = 1024
    shard = width // (gathered.shape[0] // 128 // tenants)
    frozen_cols = q_cols + d_cols
    four = gathered.reshape(width // shard, tenants, shard // tenants, gathered.shape[1])
    per = block // shard
    pack = gathered.shape[1] - frozen_cols
    rows = 32
    grid_spec = pltpu.PrefetchScalarGridSpec(
        num_scalar_prefetch=1,
        grid=(width // block,),
        in_specs=[
            pl.BlockSpec((seq, block), lambda k, w: (0, k)),
            pl.BlockSpec((seq, block), lambda k, w: (0, k)),
            pl.BlockSpec((block, frozen_cols), lambda k, w: (k, 0)),
            pl.BlockSpec((per, 1, rows, pack), lambda k, w: (k, w[0], w[1], frozen_cols // pack)),
            pl.BlockSpec((per, 1, rows, pack), lambda k, w: (k, w[0], 2 + w[1], frozen_cols // pack)),
        ],
        out_specs=[
            pl.BlockSpec((seq, q_cols), lambda k, w: (0, 0)),
            pl.BlockSpec((seq, rows), lambda k, w: (0, 0)),
            pl.BlockSpec((seq, d_cols), lambda k, w: (0, 0)),
        ],
    )
    return pl.pallas_call(
        project_kernel,
        grid_spec=grid_spec,
        out_shape=[
            jax.ShapeDtypeStruct((seq, q_cols), F32),
            jax.ShapeDtypeStruct((seq, rows), F32),
            jax.ShapeDtypeStruct((seq, d_cols), F32),
        ],
        compiler_params=params(),
        name="project",
    )(jnp.stack([tenant, slot]), tokens, cotangent, gathered, four, four)


def attend_kernel(head, scalars, qkv, low_in, dctx_in, up, context, mid, up_sum):
    seq, total = qkv.shape
    heads = total // head - 2
    q_cols = heads * head
    length = scalars[1]
    inv_root = 1.0 / jnp.sqrt(F32(head))
    low = low_in[...].astype(BF16)
    added = ADAPTER_SCALE * dot(low, up[...])
    query = (qkv[:, :q_cols] + added[:, :q_cols]).astype(BF16)
    key = qkv[:, q_cols : q_cols + head].astype(BF16)
    value = (qkv[:, q_cols + head :] + added[:, q_cols:]).astype(BF16)
    row = lax.broadcasted_iota(jnp.int32, (seq, seq), 0)
    col = lax.broadcasted_iota(jnp.int32, (seq, seq), 1)
    mask = (col <= row) & (col < length)
    keep = lax.broadcasted_iota(jnp.int32, (seq, q_cols), 0) < length
    dctx = jnp.where(keep, dctx_in[...], 0.0).astype(BF16)
    d_value = jnp.zeros((seq, head), F32)
    outs, dqs = [], []
    for h in range(heads):
        cols = slice(h * head, (h + 1) * head)
        scores = dot(query[:, cols], key, NT) * inv_root
        scores = jnp.where(mask, scores, F32(-1e30))
        top = jnp.max(scores, axis=1, keepdims=True)
        expo = jnp.where(mask, jnp.exp(scores - top), 0.0)
        probs = expo / jnp.sum(expo, axis=1, keepdims=True)
        probs_b = probs.astype(BF16)
        outs.append(dot(probs_b, value))
        d_head = dctx[:, cols]
        d_probs = dot(d_head, value, NT)
        d_value += dot(probs_b, d_head, TN)
        delta = jnp.sum(probs * d_probs, axis=1, keepdims=True)
        d_scores = (probs * (d_probs - delta)).astype(BF16)
        dqs.append(dot(d_scores, key) * inv_root)
    context[...] = jnp.where(keep, jnp.concatenate(outs, axis=1), 0.0).astype(BF16)
    d_all = jnp.concatenate(dqs + [d_value], axis=1).astype(BF16)
    mid[...] = (ADAPTER_SCALE * dot(up[...], d_all, NT)).astype(BF16)
    sums = ADAPTER_SCALE * dot(low, d_all, TN)
    rank = sums.shape[0] // 2
    slot = jnp.full((rank, head), scalars[0], jnp.int32).astype(F32)
    up_sum[...] = jnp.concatenate([sums[:rank, :q_cols], sums[rank:, q_cols:], slot], axis=1).astype(BF16)


def attend(scalars, qkv, low, dctx, up, head):
    seq, q_cols = dctx.shape
    vmem = pl.BlockSpec(memory_space=pltpu.VMEM)
    rank2 = low.shape[1]
    return pl.pallas_call(
        lambda *refs: attend_kernel(head, *refs),
        in_specs=[pl.BlockSpec(memory_space=pltpu.SMEM)] + [vmem] * 4,
        out_specs=[vmem] * 3,
        out_shape=[
            jax.ShapeDtypeStruct((seq, q_cols), BF16),
            jax.ShapeDtypeStruct((rank2, seq), BF16),
            jax.ShapeDtypeStruct((rank2 // 2, q_cols + 2 * head), BF16),
        ],
        compiler_params=params(),
        name="attend",
    )(scalars, qkv, low, dctx, up)


def term_kernel(mid, up_sum, tok, out):
    rows = mid.shape[0]
    for i in range(out.shape[0]):
        width = out.shape[2]
        out[i, :rows, :] = dot(mid[...], tok[:, i * width : (i + 1) * width]).astype(BF16)
        out[i, rows:, :] = up_sum[...]


def term(mid, up_sum, tokens, parts):
    seq, width = tokens.shape
    per = 4
    shard = width // parts
    rows = mid.shape[0] + up_sum.shape[0]
    return pl.pallas_call(
        term_kernel,
        grid=(parts // per,),
        in_specs=[
            pl.BlockSpec(mid.shape, lambda k: (0, 0)),
            pl.BlockSpec(up_sum.shape, lambda k: (0, 0)),
            pl.BlockSpec((seq, per * shard), lambda k: (0, k)),
        ],
        out_specs=pl.BlockSpec((per, rows, shard), lambda k: (k, 0, 0)),
        out_shape=jax.ShapeDtypeStruct((parts, rows, shard), BF16),
        compiler_params=params(),
        name="term",
    )(mid, up_sum, tokens)


def output_kernel(context, w, out):
    out[...] = dot(context[...], w[...], NT).astype(BF16)


def output_of(context, gathered, first, cost):
    seq, cols = context.shape
    width = gathered.shape[0]
    block = 1024
    return pl.pallas_call(
        output_kernel,
        grid=(width // block,),
        in_specs=[
            pl.BlockSpec((seq, cols), lambda k: (0, 0)),
            pl.BlockSpec((block, cols), lambda k: (k, first // cols)),
        ],
        out_specs=pl.BlockSpec((seq, block), lambda k: (0, k)),
        out_shape=jax.ShapeDtypeStruct((seq, width), BF16),
        compiler_params=params(),
        cost_estimate=cost,
        name="output",
    )(context, gathered)


def total_kernel(got, down, up):
    rows = down.shape[1]
    cols = up.shape[2]
    sums = [jnp.zeros(got.shape[1:], F32) for _ in range(2)]
    for f in range(got.shape[0]):
        part = got[f].astype(F32)
        one = part[rows : rows + 1, cols : cols + 1]
        sums[0] += part * (1.0 - one)
        sums[1] += part * one
    for s in range(2):
        down[s] = sums[s][:rows]
        up[s] = sums[s][rows:, :cols]


def total(got, rows, cols):
    parts, every, shard = got.shape
    vmem = pl.BlockSpec(memory_space=pltpu.VMEM)
    return pl.pallas_call(
        total_kernel,
        in_specs=[vmem],
        out_specs=[vmem] * 2,
        out_shape=[
            jax.ShapeDtypeStruct((2, rows, shard), F32),
            jax.ShapeDtypeStruct((2, every - rows, cols), F32),
        ],
        compiler_params=params(),
        name="total",
    )(got)


def body(
    tokens,
    cotangent,
    w_query,
    w_key,
    w_value,
    w_output,
    adapter_down,
    adapter_up,
    tenant_slot,
    lengths,
):
    seq, width = tokens.shape
    q_cols = w_query.shape[1]
    head = w_key.shape[1]
    shard, slots, _, rank = adapter_down.shape
    tenants = lax.axis_size("tenant")
    parts = lax.axis_size("fsdp")
    tenant = lax.axis_index("tenant").astype(jnp.int32)
    slot = tenant_slot[0]
    quarter = shard // tenants

    def mine(w):
        return lax.dynamic_slice_in_dim(w, tenant * quarter, quarter, 0)

    down = adapter_down.reshape(shard, slots * 2 * rank).T
    down = jnp.concatenate([down[:, : shard // 2], down[:, shard // 2 :]], axis=0)
    local = jnp.concatenate(
        [mine(w_query), mine(w_key), mine(w_value), mine(w_output.T), down], axis=1
    )
    gathered = lax.all_gather(local, ("fsdp", "tenant"), axis=0, tiled=True)
    up = lax.dynamic_index_in_dim(adapter_up, slot, 0, keepdims=False)
    at_query = jnp.arange(q_cols + head)[None, :] < q_cols
    up = jnp.concatenate(
        [jnp.where(at_query, up, 0), jnp.where(at_query, 0, up)], axis=0
    ).astype(BF16)
    qkv_cols = q_cols + 2 * head
    qkv, low, dctx = project(
        tokens, cotangent, gathered, tenant, slot, qkv_cols, q_cols, tenants
    )
    scalars = jnp.stack([slot, lengths[0]])
    context, mid, up_sum = attend(scalars, qkv, low, dctx, up, head)
    sent = term(mid, up_sum, tokens, parts)
    got = lax.all_to_all(sent, "fsdp", split_axis=0, concat_axis=0, tiled=True)
    cost = pl.CostEstimate(
        flops=2 * seq * q_cols * width, bytes_accessed=4 * seq * width, transcendentals=0
    )
    output = output_of(context, gathered, qkv_cols, cost)
    down_sum, grad_up = total(got, 2 * rank, q_cols + head)
    grad_down = down_sum.reshape(slots * 2 * rank, shard).T.reshape(shard, slots, 2, rank)
    return (output, grad_down, grad_up)


def solution(mesh):
    placed = (
        P(("fsdp", "tenant"), None),
        P(("fsdp", "tenant"), None),
        P("fsdp", None),
        P("fsdp", None),
        P("fsdp", None),
        P(None, "fsdp"),
        P("fsdp", "tenant", None, None),
        P("tenant", None, None),
        P(("fsdp", "tenant")),
        P(("fsdp", "tenant")),
    )
    return jax.shard_map(
        body,
        mesh=mesh,
        in_specs=placed,
        out_specs=(
            P(("fsdp", "tenant"), None),
            P("fsdp", "tenant", None, None),
            P("tenant", None, None),
        ),
        check_vma=False,
    )
```

time: 693 us -> 197 us (0.28)
  waiting for transfers between devices: 436 us -> 120 us
  blocking collectives: 183 us -> 0 us
  matrix products: 56.7 us -> 0 us
  Pallas kernels: 0 us -> 47.2 us
    all_gather x5 -> x1, waiting for transfers between devices: 428 us -> 107 us  [body(): gathered = lax.all_gather(local, ('fsdp', 'tenant'), axis=0, tiled=True)]
    psum x1 -> x0, blocking collectives: 183 us -> none  [body(): grad_up = lax.psum(up_summand, 'fsdp')]
    dot_general x23 -> x0, matrix products: 56.7 us -> none  [the longest x1 9.21 us: body(): jnp.dot(context, lax.all_gather(w_output, 'fsdp', axis=1, tiled=True), pr...]
    pallas_call x0 -> x5, Pallas kernels: none -> 47.2 us  [the longest x1 22.4 us: project(): pl.pallas_call(project_kernel, grid_spec=grid_spec, out_shape=[jax.ShapeD...]
    all_to_all x0 -> x1, waiting for transfers between devices: none -> 13.1 us  [body(): got = lax.all_to_all(sent, 'fsdp', split_axis=0, concat_axis=0, tiled=True)]
  transfers between devices with their start and end apart: 6 -> 2, of which waited for: 6 -> 2; matrix products, arithmetic and copies ran while one was open for 6% -> 0% of each run, Pallas kernels for 0% -> 7%
where the time goes in v1:
time: 197 us; the launch traced here: 195 us
  waiting for transfers between devices  120 us (61%)
  Pallas kernels  47.2 us (24%)
  between operations  15.4 us (8%)
  starting transfers between devices  6.9 us (4%)
  local copies, waits for them, and re-layouts  4.89 us (2%)
    all_gather x1, waiting for transfers between devices, body(): gathered = lax.all_gather(local, ('fsdp', 'tenant'), axis=0, tiled=True)  107 us
    pallas_call x1, Pallas kernels, project(): pl.pallas_call(project_kernel, grid_spec=grid_spec, out_shape=[jax.ShapeD...  22.4 us
    pallas_call x1, Pallas kernels, output_of(): pl.pallas_call(output_kernel, grid=(width // block,), in_specs=[pl.BlockS...  14 us
    all_to_all x1, waiting for transfers between devices, body(): got = lax.all_to_all(sent, 'fsdp', split_axis=0, concat_axis=0, tiled=True)  13.1 us
    pallas_call x1, Pallas kernels, term(): pl.pallas_call(term_kernel, grid=(parts // per,), in_specs=[pl.BlockSpec(...  7.83 us
    all_to_all x1, starting transfers between devices, body(): got = lax.all_to_all(sent, 'fsdp', split_axis=0, concat_axis=0, tiled=True)  6.86 us
    unnamed x9, local copies, waits for them, and re-layouts  4.09 us
  transfers between devices with their start and end apart: 2, of which 2 were waited for; matrix products, arithmetic and copies ran while one was open for 0% of the time, Pallas kernels for 7%

profile of v1, /device:TPU:2, one launch (start us, length us, event | category | flops | bytes accessed | tf_op | source)
XLA Modules:
  0.0 195.5 jit_solution(7526581183453695401)
XLA Ops:
  7.2 0.0 copy-start
  7.2 0.0 all-gather.2.cloned.1.call-start
  7.2 0.9 copy-done
  8.1 0.1 copy.14
  8.2 0.8 fusion
  9.0 0.8 dynamic-slice_dynamic-update-slice_fusion
  9.9 0.8 dynamic-slice_dynamic-update-slice_fusion.2
  10.6 0.8 dynamic-slice_dynamic-update-slice_fusion.1
  11.4 0.0 copy-start.1
  11.5 0.7 copy-done.1
  12.1 0.0 all-gather.2.cloned.1.call-update
  13.5 0.1 pad_add_fusion
  13.6 0.7 bitcast_select_fusion.1
  14.3 107.1 %all-gather.2.cloned.1.call-done.frozen.w = bf16[16384,1024]{1,0:T(8,128)(2,1)} async-done(((bf16[128,1024]{1,0:T(8,128)(2,1)}), bf16[16384,1024]{1,0:T(8,128)(2,1)}) %all-gather.2.cloned.1.call-update) | async-done | bytes 33554448 | tf_op jit(solution)/shard_map/all_gather | solution.py:250
  121.4 22.4 %project.1 = (f32[256,512]{1,0:T(8,128)S(1)}, f32[256,32]{1,0:T(8,128)S(1)}, f32[256,256]{1,0:T(8,128)S(1)}) custom-call(s32[2]{0:T(128)S(1)} %get-tuple-element.24.where, bf16[256,16384]{1,0:T(8,128)(2,1)} %tok.3, bf16[256,16384]{1,0:T(8,128)(2,1)} %cot.1, bf16[16384,1024]{1,0:T(8,128)(2,1)} %all-gather.2.cloned.1.call-done.frozen.w, ...), custom_call_target="tpu_custom_call" | custom-call | tf_op jit(solution)/shard_map/project/pallas_call | solution.py:66
  143.9 1.7 attend.1
  145.6 7.8 %term.1 = bf16[32,48,512]{2,1,0:T(8,128)(2,1)} custom-call(bf16[32,256]{1,0:T(8,128)(2,1)S(1)} %get-tuple-element.15.mid, bf16[16,512]{1,0:T(8,128)(2,1)S(1)} %get-tuple-element.16.up_sum, bf16[256,16384]{1,0:T(8,128)(2,1)} %tok.3), custom_call_target="tpu_custom_call" | custom-call | tf_op jit(solution)/shard_map/term/pallas_call | solution.py:152
  153.4 6.9 %all-to-all-start = ((bf16[32,48,512]{2,1,0:T(8,128)(2,1)}), bf16[32,48,512]{2,1,0:T(8,128)(2,1)S(1)}, u32[]{:S(2)}, u32[]{:S(2)}) async-start(bf16[32,48,512]{2,1,0:T(8,128)(2,1)} %term.1), calls=%async_computation | async-start | bytes 3145728 | tf_op jit(solution)/shard_map/all_to_all | solution.py:263
  160.3 14.0 %output.1 = bf16[256,16384]{1,0:T(8,128)(2,1)} custom-call(bf16[256,256]{1,0:T(8,128)(2,1)S(1)} %get-tuple-element.14.context, bf16[16384,1024]{1,0:T(8,128)(2,1)} %all-gather.2.cloned.1.call-done.frozen.w), custom_call_target="tpu_custom_call" | custom-call | flops 2147483648 | bytes 16777216 | tf_op jit(solution)/shard_map/output/pallas_call | solution.py:175
  174.3 13.1 %all-to-all-done.got = bf16[32,48,512]{2,1,0:T(8,128)(2,1)S(1)} async-done(((bf16[32,48,512]{2,1,0:T(8,128)(2,1)}), bf16[32,48,512]{2,1,0:T(8,128)(2,1)S(1)}, u32[]{:S(2)}, u32[]{:S(2)}) %all-to-all-start) | async-done | bytes 1572896 | tf_op jit(solution)/shard_map/all_to_all | solution.py:263
  187.4 1.2 total.1
  (5 shorter events, 0.0 us)
Async XLA Ops:
  7.2 1.0 copy-start
  7.2 114.3 %all-gather.2.cloned.1.call-start = ((), (), s32[]{:S(2)}) async-start(), calls=%async_computation.1 | async-start | bytes 33816576 | tf_op jit(solution)/shard_map/all_gather | solution.py:250
  11.4 0.7 copy-start.1
  153.4 34.0 %all-to-all-start = ((bf16[32,48,512]{2,1,0:T(8,128)(2,1)}), bf16[32,48,512]{2,1,0:T(8,128)(2,1)S(1)}, u32[]{:S(2)}, u32[]{:S(2)}) async-start(bf16[32,48,512]{2,1,0:T(8,128)(2,1)} %term.1), calls=%async_computation | async-start | bytes 3145728 | tf_op jit(solution)/shard_map/all_to_all | solution.py:263
Sparse Core Ops, SparseCore 0:
  12.3 109.0 all-gather.1

commit v2 on v1

v2 whole, which is shorter than its diff:
```python
import functools

import jax
import jax.numpy as jnp
from jax import lax
from jax.experimental import pallas as pl
from jax.experimental.pallas import tpu as pltpu
from jax.sharding import PartitionSpec as P

ADAPTER_SCALE = 2.0
Y, Z = 4, 4
VMEM = 48 * 1024 * 1024
NT = (((1,), (1,)), ((), ()))
TN = (((0,), (0,)), ((), ()))
F32 = jnp.float32
BF16 = jnp.bfloat16


def dot(a, b, dims=(((1,), (0,)), ((), ()))):
    return lax.dot_general(a, b, dims, preferred_element_type=F32)


def params(**kw):
    return pltpu.CompilerParams(vmem_limit_bytes=VMEM, **kw)


def pack_kernel(where, w_query, w_key, w_value, down, w_output, out):
    head, low = w_key.shape[1], down.shape[0]
    half = out.shape[1]
    out[:half, :] = w_query[...]
    out[half : 2 * half, :head] = w_key[...]
    out[half : 2 * half, head:] = w_value[...]
    for h in range(2):
        out[2 * half + h * low : 2 * half + (h + 1) * low, :] = down[:, h * half : (h + 1) * half]
    out[2 * half + 2 * low :, :] = w_output[...]


def pack(where, w_query, w_key, w_value, down, w_output):
    half = w_query.shape[0] // 2
    q_cols, head, low = w_query.shape[1], w_key.shape[1], down.shape[0]
    rows = lambda cols: pl.BlockSpec((half, cols), lambda k, w: (w[0], 0))
    return pl.pallas_call(
        pack_kernel,
        grid_spec=pltpu.PrefetchScalarGridSpec(
            num_scalar_prefetch=1,
            grid=(1,),
            in_specs=[
                rows(q_cols),
                rows(head),
                rows(head),
                pl.BlockSpec(down.shape, lambda k, w: (0, 0)),
                pl.BlockSpec((q_cols, half), lambda k, w: (0, w[0])),
            ],
            out_specs=pl.BlockSpec((3 * half + 2 * low, half), lambda k, w: (0, 0)),
        ),
        out_shape=jax.ShapeDtypeStruct((3 * half + 2 * low, half), BF16),
        compiler_params=params(),
        name="pack",
    )(where, w_query, w_key, w_value, down, w_output)


def pick_kernel(where, a, b, out_a, out_b):
    piece = 256
    for side in range(2):

        @pl.when(where[0] == side)
        def _():
            for full, out in ((a, out_a), (b, out_b)):
                for i in range(out.shape[1] // piece):
                    at = (2 * i + 1 - side) * piece
                    out[:, i * piece : (i + 1) * piece] = full[:, at : at + piece]


def pick(a, b, where):
    seq, width = a.shape
    block = 4096
    return pl.pallas_call(
        pick_kernel,
        grid_spec=pltpu.PrefetchScalarGridSpec(
            num_scalar_prefetch=1,
            grid=(width // block,),
            in_specs=[pl.BlockSpec((seq, block), lambda k, w: (0, k))] * 2,
            out_specs=[pl.BlockSpec((seq, block // 2), lambda k, w: (0, k))] * 2,
        ),
        out_shape=[jax.ShapeDtypeStruct((seq, width // 2), BF16)] * 2,
        compiler_params=params(),
        cost_estimate=pl.CostEstimate(flops=0, bytes_accessed=6 * seq * width, transcendentals=0),
        name="pick",
    )(where, a, b)


def arrive_kernel(where, tok, cot_a, cot_b, mate_tok, mate_cot, near, far, *refs, fresh):
    *after, kept = refs[-4:]
    step = pl.program_id(0)

    @pl.when(step == 0)
    def _():
        for i, new in enumerate(after):
            new[...] = jnp.zeros_like(new) if fresh else refs[i][...]

    mine, other, low = after
    core, slot, x_hi = where[0], where[1], where[2]
    half = near.shape[3]
    first = near.shape[2] - half

    def add(pair):
        own = jnp.concatenate(
            [tok[:, pl.ds(pl.multiple_of((2 * x + core) * half, half), half)] for x in range(2)], axis=1
        )
        at = [x ^ x_hi for x in range(2)]
        for g in range(2):
            cols = slice(g * half, (g + 1) * half)
            w = jnp.concatenate([pair[0, i, cols, :] for i in at], axis=0)
            mine[:, cols] += dot(own, w)
            other[:, cols] += dot(mate_tok[...], w)
        w = [pair[0, i, first:, :] for i in at]
        cols = slice(2 * half, 3 * half)
        both = jnp.concatenate(w, axis=1)
        mine[:, cols] += dot(jnp.concatenate([cot_a[...], cot_b[...]], axis=1), both, NT)
        other[:, cols] += dot(mate_cot[...], both, NT)
        for x in range(2):
            kept[0, x] = w[x]
        down = [
            pair[0, i, pl.ds(pl.multiple_of(2 * half + h * 64 + slot * 32, 32), 32), :]
            for i in at
            for h in range(2)
        ]
        low[...] += dot(tok[...], jnp.concatenate(down, axis=1), NT)

    count = pl.num_programs(0) // 2

    @pl.when(step < count)
    def _():
        add(near)

    @pl.when(step >= count)
    def _():
        add(far)


def arrive(where, tokens, cotangent, mate_tok, mate_cot, first, second, sums, out_shape):
    seq = tokens.shape[0]
    count, _, rows, half = first[0].shape
    steps = first[1] + second[1]

    def at(k, w):
        early = jnp.int32(steps[0])
        for i in range(1, len(steps)):
            early = jnp.where(k == i, steps[i], early)
        late = jnp.where(k < count, first[2], second[2])
        y = (w[3] - jnp.where(w[0] == 0, late, early) + Y) % Y
        z = (w[4] - jnp.where(w[0] == 0, early, late) + Z) % Z
        return y * Z + z

    whole = [pl.BlockSpec(x.shape, lambda k, w: (0, 0)) for x in out_shape[:3]]
    block = (1, 2, rows, half)
    fresh = not sums
    return pl.pallas_call(
        functools.partial(arrive_kernel, fresh=fresh),
        grid_spec=pltpu.PrefetchScalarGridSpec(
            num_scalar_prefetch=1,
            grid=(2 * count,),
            in_specs=[
                pl.BlockSpec((seq, 4 * half), lambda k, w: (0, at(k, w))),
                pl.BlockSpec((seq, half), lambda k, w: (0, 4 * at(k, w) + w[0])),
                pl.BlockSpec((seq, half), lambda k, w: (0, 4 * at(k, w) + 2 + w[0])),
                pl.BlockSpec((seq, 2 * half), lambda k, w: (0, at(k, w))),
                pl.BlockSpec((seq, 2 * half), lambda k, w: (0, at(k, w))),
                pl.BlockSpec(block, lambda k, w: (jnp.minimum(k, count - 1), 0, 0, 0)),
                pl.BlockSpec(block, lambda k, w: (jnp.maximum(k - count, 0), 0, 0, 0)),
            ]
            + ([] if fresh else whole + [pl.BlockSpec(memory_space=pl.ANY)]),
            out_specs=whole + [pl.BlockSpec((1, 2, half, half), lambda k, w: (at(k, w), 0, 0, 0))],
        ),
        out_shape=out_shape,
        input_output_aliases={} if fresh else {11: 3},
        compiler_params=params(),
        cost_estimate=pl.CostEstimate(flops=count * 2**30, bytes_accessed=count * 2**22, transcendentals=0),
        name="arrive",
    )(where, tokens, cotangent, cotangent, mate_tok, mate_cot, first[0], second[0], *sums)


def attend_kernel(head, scalars, mine, other, low_in, up, context, mid, up_sum):
    seq, total = mine.shape
    q_cols = (total - 2 * head) // 2
    heads = q_cols // head
    length = scalars[1]
    inv_root = 1.0 / jnp.sqrt(F32(head))
    low = low_in[...].astype(BF16)
    added = ADAPTER_SCALE * dot(low, up[...])
    summed = mine[...] + other[...]
    qkv, dctx = summed[:, : total - q_cols], summed[:, total - q_cols :]
    query = (qkv[:, :q_cols] + added[:, :q_cols]).astype(BF16)
    key = qkv[:, q_cols : q_cols + head].astype(BF16)
    value = (qkv[:, q_cols + head :] + added[:, q_cols:]).astype(BF16)
    row = lax.broadcasted_iota(jnp.int32, (seq, seq), 0)
    col = lax.broadcasted_iota(jnp.int32, (seq, seq), 1)
    mask = (col <= row) & (col < length)
    keep = lax.broadcasted_iota(jnp.int32, (seq, q_cols), 0) < length
    dctx = jnp.where(keep, dctx, 0.0).astype(BF16)
    d_value = jnp.zeros((seq, head), F32)
    outs, dqs = [], []
    for h in range(heads):
        cols = slice(h * head, (h + 1) * head)
        scores = dot(query[:, cols], key, NT) * inv_root
        scores = jnp.where(mask, scores, F32(-1e30))
        top = jnp.max(scores, axis=1, keepdims=True)
        expo = jnp.where(mask, jnp.exp(scores - top), 0.0)
        probs = expo / jnp.sum(expo, axis=1, keepdims=True)
        probs_b = probs.astype(BF16)
        outs.append(dot(probs_b, value))
        d_head = dctx[:, cols]
        d_probs = dot(d_head, value, NT)
        d_value += dot(probs_b, d_head, TN)
        delta = jnp.sum(probs * d_probs, axis=1, keepdims=True)
        d_scores = (probs * (d_probs - delta)).astype(BF16)
        dqs.append(dot(d_scores, key) * inv_root)
    context[...] = jnp.where(keep, jnp.concatenate(outs, axis=1), 0.0).astype(BF16)
    d_all = jnp.concatenate(dqs + [d_value], axis=1).astype(BF16)
    mid[...] = (ADAPTER_SCALE * dot(up[...], d_all, NT)).astype(BF16)
    sums = ADAPTER_SCALE * dot(low, d_all, TN)
    rank = sums.shape[0] // 2
    slot = jnp.full((rank, head), scalars[0], jnp.int32).astype(F32)
    up_sum[...] = jnp.concatenate([sums[:rank, :q_cols], sums[rank:, q_cols:], slot], axis=1).astype(BF16)


def attend(scalars, mine, other, low, up, head):
    seq, total = mine.shape
    q_cols = (total - 2 * head) // 2
    vmem = pl.BlockSpec(memory_space=pltpu.VMEM)
    rank2 = low.shape[1]
    return pl.pallas_call(
        lambda *refs: attend_kernel(head, *refs),
        in_specs=[pl.BlockSpec(memory_space=pltpu.SMEM)] + [vmem] * 4,
        out_specs=[vmem] * 3,
        out_shape=[
            jax.ShapeDtypeStruct((seq, q_cols), BF16),
            jax.ShapeDtypeStruct((rank2, seq), BF16),
            jax.ShapeDtypeStruct((rank2 // 2, q_cols + 2 * head), BF16),
        ],
        compiler_params=params(),
        name="attend",
    )(scalars, mine, other, low, up)


def term_kernel(mid, up_sum, tok, out):
    rows = mid.shape[0]
    for i in range(out.shape[0]):
        width = out.shape[2]
        out[i, :rows, :] = dot(mid[...], tok[:, i * width : (i + 1) * width]).astype(BF16)
        out[i, rows:, :] = up_sum[...]


def term(mid, up_sum, tokens, parts):
    seq, width = tokens.shape
    per = 8
    shard = width // parts
    rows = mid.shape[0] + up_sum.shape[0]
    return pl.pallas_call(
        term_kernel,
        grid=(parts // per,),
        in_specs=[
            pl.BlockSpec(mid.shape, lambda k: (0, 0)),
            pl.BlockSpec(up_sum.shape, lambda k: (0, 0)),
            pl.BlockSpec((seq, per * shard), lambda k: (0, k)),
        ],
        out_specs=pl.BlockSpec((per, rows, shard), lambda k: (k, 0, 0)),
        out_shape=jax.ShapeDtypeStruct((parts, rows, shard), BF16),
        compiler_params=params(),
        name="term",
    )(mid, up_sum, tokens)


def output_kernel(where, context, own, theirs, out):
    pairs, _, rows, half = own.shape
    for core in range(2):

        @pl.when(where[0] == core)
        def _():
            halves = (own, theirs) if core == 0 else (theirs, own)
            for p in range(pairs):
                for x in range(2):
                    w = jnp.concatenate([h[p, x] for h in halves], axis=1)
                    at = (2 * p + x) * 2 * half
                    out[:, at : at + 2 * half] = dot(context[...], w).astype(BF16)


def output_of(where, context, own, theirs, cost):
    seq, cols = context.shape
    count, _, rows, half = own.shape
    per = 2
    weights = pl.BlockSpec((per, 2, rows, half), lambda k, w: (k, 0, 0, 0))
    return pl.pallas_call(
        output_kernel,
        grid_spec=pltpu.PrefetchScalarGridSpec(
            num_scalar_prefetch=1,
            grid=(count // per,),
            in_specs=[pl.BlockSpec((seq, cols), lambda k, w: (0, 0)), weights, weights],
            out_specs=pl.BlockSpec((seq, per * 4 * half), lambda k, w: (0, k)),
        ),
        out_shape=jax.ShapeDtypeStruct((seq, count * 4 * half), BF16),
        compiler_params=params(),
        cost_estimate=cost,
        name="output",
    )(where, context, own, theirs)


def total_kernel(got, down, up):
    rows = down.shape[1]
    cols = up.shape[2]
    sums = [jnp.zeros(got.shape[1:], F32) for _ in range(2)]
    for f in range(got.shape[0]):
        part = got[f].astype(F32)
        one = part[rows : rows + 1, cols : cols + 1]
        sums[0] += part * (1.0 - one)
        sums[1] += part * one
    for s in range(2):
        down[s] = sums[s][:rows]
        up[s] = sums[s][rows:, :cols]


def total(got, rows, cols):
    parts, every, shard = got.shape
    vmem = pl.BlockSpec(memory_space=pltpu.VMEM)
    return pl.pallas_call(
        total_kernel,
        in_specs=[vmem],
        out_specs=[vmem] * 2,
        out_shape=[
            jax.ShapeDtypeStruct((2, rows, shard), F32),
            jax.ShapeDtypeStruct((2, every - rows, cols), F32),
        ],
        compiler_params=params(),
        name="total",
    )(got)


def body(
    tokens,
    cotangent,
    w_query,
    w_key,
    w_value,
    w_output,
    adapter_down,
    adapter_up,
    tenant_slot,
    lengths,
):
    seq, width = tokens.shape
    q_cols = w_query.shape[1]
    head = w_key.shape[1]
    shard, slots, _, rank = adapter_down.shape
    tenants = lax.axis_size("tenant")
    parts = lax.axis_size("fsdp")
    tenant = lax.axis_index("tenant").astype(jnp.int32)
    slot = tenant_slot[0]

    place = lax.axis_index("fsdp").astype(jnp.int32)
    y, z, x_hi = place // (2 * Z), place // 2 % Z, place % 2
    core = tenant % 2

    def shift(array, hops, late):
        to = []
        for f in range(parts):
            for t in range(tenants):
                along_y = (t % 2 == 0) == late
                f_y = (f // (2 * Z) + hops * along_y) % Y
                f_z = (f // 2 + hops * (not along_y)) % Z
                to.append((f * tenants + t, ((f_y * Z + f_z) * 2 + f % 2) * tenants + t))
        return lax.ppermute(array, ("fsdp", "tenant"), to)

    def swap(array):
        return lax.ppermute(array, "tenant", [(t, t ^ 1) for t in range(tenants)])

    where = jnp.stack([core, slot, x_hi, y, z])
    down = adapter_down.reshape(shard, slots * 2 * rank).T
    piece = pack(where, w_query, w_key, w_value, down, w_output)
    flipped = lax.ppermute(piece, "fsdp", [(f, f ^ 1) for f in range(parts)])
    hops = (1, 3, 2)
    early = {j: shift(piece, j, False) for j in hops}
    halves = pick(tokens, cotangent, where)
    flipped, early, halves = lax.optimization_barrier((flipped, early, halves))
    early_flipped = {j: shift(flipped, j, False) for j in hops}
    mate_tok, mate_cot = (swap(half) for half in halves)
    early[0], early_flipped[0] = piece, flipped

    def group(steps):
        return jnp.stack([jnp.stack([early[j], early_flipped[j]]) for j in steps])

    near, far = (0, 1), (3, 2)
    here_near, here_far = group(near), group(far)
    ahead_near, behind_far = shift(here_near, 1, True), shift(here_far, -1, True)
    ahead_far, behind_near = shift(here_far, 1, True), shift(here_near, -1, True)
    out_shape = [jax.ShapeDtypeStruct((seq, 2 * (q_cols + head)), F32)] * 2 + [
        jax.ShapeDtypeStruct((seq, 2 * rank), F32),
        jax.ShapeDtypeStruct((parts // 2, 2, q_cols, shard // 2), BF16),
    ]

    def add(first, second, sums):
        return arrive(where, tokens, cotangent, mate_tok, mate_cot, first, second, sums, out_shape)

    sums = add((here_near, near, 0), (here_far, far, 0), ())
    ahead_near, behind_far, sums = lax.optimization_barrier((ahead_near, behind_far, sums))
    far_ahead, far_behind = shift(ahead_near, 1, True), shift(behind_far, -1, True)
    sums = add((ahead_near, near, 1), (behind_far, far, 3), sums)
    sums = add((ahead_far, far, 1), (behind_near, near, 3), sums)
    sums = add((far_ahead, near, 2), (far_behind, far, 2), sums)
    summed, other, low, kept = sums
    other = swap(other)
    other, kept = lax.optimization_barrier((other, kept))
    theirs = swap(kept)

    up = lax.dynamic_index_in_dim(adapter_up, slot, 0, keepdims=False)
    at_query = jnp.arange(q_cols + head)[None, :] < q_cols
    up = jnp.concatenate(
        [jnp.where(at_query, up, 0), jnp.where(at_query, 0, up)], axis=0
    ).astype(BF16)
    scalars = jnp.stack([slot, lengths[0]])
    context, mid, up_sum = attend(scalars, summed, other, low, up, head)
    sent = term(mid, up_sum, tokens, parts)
    got = lax.all_to_all(sent, "fsdp", split_axis=0, concat_axis=0, tiled=True)
    cost = pl.CostEstimate(
        flops=2 * seq * q_cols * width, bytes_accessed=4 * seq * width, transcendentals=0
    )
    output = output_of(where, context, kept, theirs, cost)
    got, output = lax.optimization_barrier((got, output))
    down_sum, grad_up = total(got, 2 * rank, q_cols + head)
    grad_down = down_sum.reshape(slots * 2 * rank, shard).T.reshape(shard, slots, 2, rank)
    return (output, grad_down, grad_up)


def solution(mesh):
    placed = (
        P(("fsdp", "tenant"), None),
        P(("fsdp", "tenant"), None),
        P("fsdp", None),
        P("fsdp", None),
        P("fsdp", None),
        P(None, "fsdp"),
        P("fsdp", "tenant", None, None),
        P("tenant", None, None),
        P(("fsdp", "tenant")),
        P(("fsdp", "tenant")),
    )
    return jax.shard_map(
        body,
        mesh=mesh,
        in_specs=placed,
        out_specs=(
            P(("fsdp", "tenant"), None),
            P("fsdp", "tenant", None, None),
            P("tenant", None, None),
        ),
        check_vma=False,
    )
```

time: 197 us -> 161 us (0.82)
  waiting for transfers between devices: 120 us -> 64.1 us
  starting transfers between devices: 6.9 us -> 30.2 us
  between operations: 15.4 us -> 2.1 us
  Pallas kernels: 47.2 us -> 55.7 us
  local copies, waits for them, and re-layouts: 4.89 us -> 7.13 us
    all_gather x1 -> x0, waiting for transfers between devices: 107 us -> none  [body(): gathered = lax.all_gather(local, ('fsdp', 'tenant'), axis=0, tiled=True)]
    ppermute x0 -> x17, waiting for transfers between devices: none -> 47.8 us  [the longest x12 45.5 us: shift(): return lax.ppermute(array, ('fsdp', 'tenant'), to)]
    ppermute x0 -> x17, starting transfers between devices: none -> 24.5 us  [the longest x12 21.6 us: shift(): return lax.ppermute(array, ('fsdp', 'tenant'), to)]
    pallas_call x2 -> x7, Pallas kernels: 36.5 us -> 46.9 us  [the longest x4 28.4 us: arrive(): pl.pallas_call(functools.partial(arrive_kernel, fresh=fresh), grid_spec=p...]
    all_to_all x1, waiting for transfers between devices: 13.1 us -> 16.3 us  [body(): got = lax.all_to_all(sent, 'fsdp', split_axis=0, concat_axis=0, tiled=True)]
    unnamed x9 -> x18, local copies, waits for them, and re-layouts: 4.09 us -> 7.04 us
  transfers between devices with their start and end apart: 2 -> 18, of which waited for: 2 -> 9; matrix products, arithmetic and copies ran while one was open for 0% -> 0% of each run, Pallas kernels for 7% -> 29%
where the time goes in v2:
time: 161 us; the launch traced here: 160 us
  waiting for transfers between devices  64.1 us (40%)
  Pallas kernels  55.7 us (35%)
  starting transfers between devices  30.2 us (19%)
  local copies, waits for them, and re-layouts  7.13 us (4%)
  between operations  2.1 us (1%)
    ppermute x12, waiting for transfers between devices, shift(): return lax.ppermute(array, ('fsdp', 'tenant'), to)  45.5 us
    pallas_call x4, Pallas kernels, arrive(): pl.pallas_call(functools.partial(arrive_kernel, fresh=fresh), grid_spec=p...  28.4 us
    ppermute x12, starting transfers between devices, shift(): return lax.ppermute(array, ('fsdp', 'tenant'), to)  21.6 us
    all_to_all x1, waiting for transfers between devices, body(): got = lax.all_to_all(sent, 'fsdp', split_axis=0, concat_axis=0, tiled=True)  16.3 us
    pallas_call x1, Pallas kernels, output_of(): pl.pallas_call(output_kernel, grid_spec=pltpu.PrefetchScalarGridSpec(num_...  9.3 us
    pallas_call x1, Pallas kernels, pick(): pl.pallas_call(pick_kernel, grid_spec=pltpu.PrefetchScalarGridSpec(num_sc...  8.57 us
    unnamed x18, local copies, waits for them, and re-layouts  7.04 us
    pallas_call x1, Pallas kernels, term(): pl.pallas_call(term_kernel, grid=(parts // per,), in_specs=[pl.BlockSpec(...  5.91 us
  transfers between devices with their start and end apart: 18, of which 9 were waited for; matrix products, arithmetic and copies ran while one was open for 0% of the time, Pallas kernels for 29%

profile of v2, /device:TPU:2, one launch (start us, length us, event | category | flops | bytes accessed | tf_op | source)
XLA Modules:
  0.0 160.0 jit_solution(12289008501040548592)
XLA Ops:
  1.4 0.9 copy-done.1
  2.4 0.9 copy-done.2
  3.3 0.9 copy-done.3
  4.2 0.9 copy-done.4
  5.1 0.8 copy-done.5
  6.0 0.6 pack.1
  6.6 2.2 %collective-permute-start = (bf16[896,256]{1,0:T(8,128)(2,1)S(1)}, bf16[896,256]{1,0:T(8,128)(2,1)S(1)}, u32[]{:S(2)}, u32[]{:S(2)}) collective-permute-start(bf16[896,256]{1,0:T(8,128)(2,1)S(1)} %pack.1), channel_id=1, source_target_pairs={{0,4},{4,0},{8,12},{12,8},{16,20},{20,16},{24,28},{28,24},{32,36},... | collective-permute-start | bytes 1376264 | tf_op jit(solution)/shard_map/ppermute | solution.py:379
  8.8 1.9 %collective-permute-start.1 = (bf16[896,256]{1,0:T(8,128)(2,1)S(1)}, bf16[896,256]{1,0:T(8,128)(2,1)S(1)}, u32[]{:S(2)}, u32[]{:S(2)}) collective-permute-start(bf16[896,256]{1,0:T(8,128)(2,1)S(1)} %pack.1), channel_id=1, source_target_pairs={{0,8},{1,33},{2,10},{3,35},{4,12},{5,37},{6,14},{7,39},{8,16},{9,4... | collective-permute-start | bytes 1376264 | tf_op jit(solution)/shard_map/ppermute | solution.py:371
  10.7 3.6 %collective-permute-start.2 = (bf16[896,256]{1,0:T(8,128)(2,1)S(1)}, bf16[896,256]{1,0:T(8,128)(2,1)S(1)}, u32[]{:S(2)}, u32[]{:S(2)}) collective-permute-start(bf16[896,256]{1,0:T(8,128)(2,1)S(1)} %pack.1), channel_id=1, source_target_pairs={{0,16},{1,65},{2,18},{3,67},{4,20},{5,69},{6,22},{7,71},{8,24},{9,... | collective-permute-start | bytes 1376264 | tf_op jit(solution)/shard_map/ppermute | solution.py:371
  14.3 1.0 collective-permute-start.3
  15.3 8.6 %pick.1 = (bf16[256,8192]{1,0:T(8,128)(2,1)S(1)}, bf16[256,8192]{1,0:T(8,128)(2,1)}) custom-call(s32[5]{0:T(128)S(1)} %stack.77.where, bf16[256,16384]{1,0:T(8,128)(2,1)} %tok.9, bf16[256,16384]{1,0:T(8,128)(2,1)} %cot_b.7), custom_call_target="tpu_custom_call" | custom-call | bytes 25165824 | tf_op jit(solution)/shard_map/pick/pallas_call | solution.py:77
  23.8 1.8 %collective-permute-done.2 = bf16[896,256]{1,0:T(8,128)(2,1)S(1)} collective-permute-done((bf16[896,256]{1,0:T(8,128)(2,1)S(1)}, bf16[896,256]{1,0:T(8,128)(2,1)S(1)}, u32[]{:S(2)}, u32[]{:S(2)}) %collective-permute-start.2) | collective-permute-done | bytes 458784 | tf_op jit(solution)/shard_map/ppermute | solution.py:371
  25.6 0.5 collective-permute-start.5
  26.1 2.1 %collective-permute-start.8 = (bf16[896,256]{1,0:T(8,128)(2,1)S(1)}, bf16[896,256]{1,0:T(8,128)(2,1)S(1)}, u32[]{:S(2)}, u32[]{:S(2)}) collective-permute-start(bf16[896,256]{1,0:T(8,128)(2,1)S(1)} %collective-permute-done), channel_id=1, source_target_pairs={{0,24},{1,97},{2,26},{3,99},{4,28},{5,101},{6,30},{7,103},{8,0},{9... | collective-permute-start | bytes 1376264 | tf_op jit(solution)/shard_map/ppermute | solution.py:371
  28.2 1.4 collective-permute-start.9
  29.6 0.4 collective-permute-start.6
  30.1 0.1 maximum_bitcast_fusion
  30.2 9.0 %collective-permute-done.8 = bf16[896,256]{1,0:T(8,128)(2,1)S(1)} collective-permute-done((bf16[896,256]{1,0:T(8,128)(2,1)S(1)}, bf16[896,256]{1,0:T(8,128)(2,1)S(1)}, u32[]{:S(2)}, u32[]{:S(2)}) %collective-permute-start.8) | collective-permute-done | bytes 458784 | tf_op jit(solution)/shard_map/ppermute | solution.py:371
  39.2 0.1 maximum_bitcast_fusion.2
  39.3 0.1 maximum_bitcast_fusion.3
  39.3 0.2 pad_maximum_fusion.1.far
  39.5 3.1 %collective-permute-start.10 = (bf16[2,2,896,256]{3,2,1,0:T(8,128)(2,1)S(1)}, bf16[2,2,896,256]{3,2,1,0:T(8,128)(2,1)S(1)}, u32[]{:S(2)}, u32[]{:S(2)}) collective-permute-start(bf16[2,2,896,256]{3,2,1,0:T(8,128)(2,1)S(1)} %pad_maximum_fusion.1.far), channel_id=1, source_target_pairs={{0,96},{1,25},{2,98},{3,27},{4,100},{5,29},{6,102},{7,31},{8,104},... | collective-permute-start | bytes 5505032 | tf_op jit(solution)/shard_map/ppermute | solution.py:371
  42.6 0.5 collective-permute-done.6
  43.1 0.1 maximum_bitcast_fusion.1
  43.2 0.2 pad_maximum_fusion.near
  43.4 1.6 %collective-permute-start.7 = (bf16[2,2,896,256]{3,2,1,0:T(8,128)(2,1)S(1)}, bf16[2,2,896,256]{3,2,1,0:T(8,128)(2,1)S(1)}, u32[]{:S(2)}, u32[]{:S(2)}) collective-permute-start(bf16[2,2,896,256]{3,2,1,0:T(8,128)(2,1)S(1)} %pad_maximum_fusion.near), channel_id=1, source_target_pairs={{0,32},{1,9},{2,34},{3,11},{4,36},{5,13},{6,38},{7,15},{8,40},{9,1... | collective-permute-start | bytes 5505032 | tf_op jit(solution)/shard_map/ppermute | solution.py:371
  45.0 1.6 collective-permute-start.13
  46.6 1.7 %collective-permute-start.14 = (bf16[2,2,896,256]{3,2,1,0:T(8,128)(2,1)S(1)}, bf16[2,2,896,256]{3,2,1,0:T(8,128)(2,1)}, u32[]{:S(2)}, u32[]{:S(2)}) collective-permute-start(bf16[2,2,896,256]{3,2,1,0:T(8,128)(2,1)S(1)} %pad_maximum_fusion.near), channel_id=1, source_target_pairs={{0,96},{1,25},{2,98},{3,27},{4,100},{5,29},{6,102},{7,31},{8,104},... | collective-permute-start | bytes 5505032 | tf_op jit(solution)/shard_map/ppermute | solution.py:371
  48.3 0.3 copy-done.6
  48.6 6.6 %arrive.4 = (f32[256,768]{1,0:T(8,128)S(1)}, f32[256,768]{1,0:T(8,128)S(1)}, f32[256,32]{1,0:T(8,128)S(1)}, bf16[16,2,256,256]{3,2,1,0:T(8,128)(2,1)}) custom-call(s32[5]{0:T(128)S(1)} %stack.77.where, bf16[256,16384]{1,0:T(8,128)(2,1)} %tok.9, bf16[256,16384]{1,0:T(8,128)(2,1)} %cot_b.7, bf16[256,16384]{1,0:T(8,128)(2,1)} %cot_b.7, ...), custom_call_target="tpu_custom_call" | custom-call | flops 2147483648 | bytes 8388608 | tf_op jit(solution)/shard_map/arrive/pallas_call | solution.py:158
  55.2 8.2 %collective-permute-done.10.far = bf16[2,2,896,256]{3,2,1,0:T(8,128)(2,1)S(1)} collective-permute-done((bf16[2,2,896,256]{3,2,1,0:T(8,128)(2,1)S(1)}, bf16[2,2,896,256]{3,2,1,0:T(8,128)(2,1)S(1)}, u32[]{:S(2)}, u32[]{:S(2)}) %collective-permute-start.10) | collective-permute-done | bytes 1835040 | tf_op jit(solution)/shard_map/ppermute | solution.py:371
  63.4 4.5 %collective-permute-done.7.near = bf16[2,2,896,256]{3,2,1,0:T(8,128)(2,1)S(1)} collective-permute-done((bf16[2,2,896,256]{3,2,1,0:T(8,128)(2,1)S(1)}, bf16[2,2,896,256]{3,2,1,0:T(8,128)(2,1)S(1)}, u32[]{:S(2)}, u32[]{:S(2)}) %collective-permute-start.7) | collective-permute-done | bytes 1835040 | tf_op jit(solution)/shard_map/ppermute | solution.py:371
  67.9 0.4 collective-permute-start.11
  68.2 2.9 %collective-permute-start.12 = (bf16[2,2,896,256]{3,2,1,0:T(8,128)(2,1)S(1)}, bf16[2,2,896,256]{3,2,1,0:T(8,128)(2,1)}, u32[]{:S(2)}, u32[]{:S(2)}) collective-permute-start(bf16[2,2,896,256]{3,2,1,0:T(8,128)(2,1)S(1)} %collective-permute-done.10.far), channel_id=1, source_target_pairs={{0,96},{1,25},{2,98},{3,27},{4,100},{5,29},{6,102},{7,31},{8,104},... | collective-permute-start | bytes 5505032 | tf_op jit(solution)/shard_map/ppermute | solution.py:371
  71.1 7.3 %arrive.5 = (f32[256,768]{1,0:T(8,128)S(1)}, f32[256,768]{1,0:T(8,128)S(1)}, f32[256,32]{1,0:T(8,128)S(1)}, bf16[16,2,256,256]{3,2,1,0:T(8,128)(2,1)}) custom-call(s32[5]{0:T(128)S(1)} %stack.77.where, bf16[256,16384]{1,0:T(8,128)(2,1)} %tok.9, bf16[256,16384]{1,0:T(8,128)(2,1)} %cot_b.7, ...), custom_call_target="tpu_custom_call", output_to_operand_aliasing={{3}: (11, {})} | custom-call | flops 2147483648 | bytes 8388608 | tf_op jit(solution)/shard_map/arrive/pallas_call | solution.py:158
  78.4 9.1 %collective-permute-done.13.near = bf16[2,2,896,256]{3,2,1,0:T(8,128)(2,1)S(1)} collective-permute-done((bf16[2,2,896,256]{3,2,1,0:T(8,128)(2,1)S(1)}, bf16[2,2,896,256]{3,2,1,0:T(8,128)(2,1)S(1)}, u32[]{:S(2)}, u32[]{:S(2)}) %collective-permute-start.13) | collective-permute-done | bytes 1835040 | tf_op jit(solution)/shard_map/ppermute | solution.py:371
  87.5 7.3 %arrive.6 = (f32[256,768]{1,0:T(8,128)S(1)}, f32[256,768]{1,0:T(8,128)S(1)}, f32[256,32]{1,0:T(8,128)S(1)}, bf16[16,2,256,256]{3,2,1,0:T(8,128)(2,1)}) custom-call(s32[5]{0:T(128)S(1)} %stack.77.where, bf16[256,16384]{1,0:T(8,128)(2,1)} %tok.9, bf16[256,16384]{1,0:T(8,128)(2,1)} %cot_b.7, ...), custom_call_target="tpu_custom_call", output_to_operand_aliasing={{3}: (11, {})} | custom-call | flops 2147483648 | bytes 8388608 | tf_op jit(solution)/shard_map/arrive/pallas_call | solution.py:158
  94.8 12.4 %collective-permute-done.11.near = bf16[2,2,896,256]{3,2,1,0:T(8,128)(2,1)S(1)} collective-permute-done((bf16[2,2,896,256]{3,2,1,0:T(8,128)(2,1)S(1)}, bf16[2,2,896,256]{3,2,1,0:T(8,128)(2,1)S(1)}, u32[]{:S(2)}, u32[]{:S(2)}) %collective-permute-start.11) | collective-permute-done | bytes 1835040 | tf_op jit(solution)/shard_map/ppermute | solution.py:371
  107.2 7.3 %arrive.7 = (f32[256,768]{1,0:T(8,128)S(1)}, f32[256,768]{1,0:T(8,128)S(1)}, f32[256,32]{1,0:T(8,128)S(1)}, bf16[16,2,256,256]{3,2,1,0:T(8,128)(2,1)}) custom-call(s32[5]{0:T(128)S(1)} %stack.77.where, bf16[256,16384]{1,0:T(8,128)(2,1)} %tok.9, bf16[256,16384]{1,0:T(8,128)(2,1)} %cot_b.7, ...), custom_call_target="tpu_custom_call", output_to_operand_aliasing={{3}: (11, {})} | custom-call | flops 2147483648 | bytes 8388608 | tf_op jit(solution)/shard_map/arrive/pallas_call | solution.py:158
  114.5 2.3 %collective-permute-done.15.refs_2_ = f32[256,768]{1,0:T(8,128)S(1)} collective-permute-done((f32[256,768]{1,0:T(8,128)S(1)}, f32[256,768]{1,0:T(8,128)S(1)}, u32[]{:S(2)}, u32[]{:S(2)}) %collective-permute-start.15) | collective-permute-done | bytes 786464 | tf_op jit(solution)/shard_map/ppermute | solution.py:374
  116.8 0.1 collective-permute-start.16
  117.7 1.7 %attend.1 = (bf16[256,256]{1,0:T(8,128)(2,1)S(1)}, bf16[32,256]{1,0:T(8,128)(2,1)S(1)}, bf16[16,512]{1,0:T(8,128)(2,1)S(1)}) custom-call(s32[2]{0:T(128)S(1)} %pad_add_fusion.refs_0_, f32[256,768]{1,0:T(8,128)S(1)} %get-tuple-element.68.refs_1_, f32[256,768]{1,0:T(8,128)S(1)} %collective-permute-done.15.refs_2_, f32[256,32]{1,0:T(8,128)S(1)} %get-tuple-element.72.refs_3_, ...), custom_call_target="tpu_custom_call" | custom-call | tf_op jit(solution)/shard_map/attend/pallas_call | solution.py:232
  119.4 5.9 %term.1 = bf16[32,48,512]{2,1,0:T(8,128)(2,1)} custom-call(bf16[32,256]{1,0:T(8,128)(2,1)S(1)} %get-tuple-element.73.mid, bf16[16,512]{1,0:T(8,128)(2,1)S(1)} %get-tuple-element.74.up_sum, bf16[256,16384]{1,0:T(8,128)(2,1)} %tok.9), custom_call_target="tpu_custom_call" | custom-call | tf_op jit(solution)/shard_map/term/pallas_call | solution.py:259
  125.3 5.7 %all-to-all-start = ((bf16[32,48,512]{2,1,0:T(8,128)(2,1)}), bf16[32,48,512]{2,1,0:T(8,128)(2,1)S(1)}, u32[]{:S(2)}, u32[]{:S(2)}) async-start(bf16[32,48,512]{2,1,0:T(8,128)(2,1)} %term.1), calls=%async_computation | async-start | bytes 3145728 | tf_op jit(solution)/shard_map/all_to_all | solution.py:422
  131.0 2.2 %copy-done = bf16[16,2,256,256]{3,2,1,0:T(8,128)(2,1)S(1)} copy-done((bf16[16,2,256,256]{3,2,1,0:T(8,128)(2,1)S(1)}, bf16[16,2,256,256]{3,2,1,0:T(8,128)(2,1)}, u32[]{:S(2)}) %copy-start) | copy-done | bytes 4194328
  133.2 9.3 %output.1 = bf16[256,16384]{1,0:T(8,128)(2,1)} custom-call(s32[5]{0:T(128)S(1)} %stack.77.where, bf16[256,256]{1,0:T(8,128)(2,1)S(1)} %get-tuple-element.75.context, bf16[16,2,256,256]{3,2,1,0:T(8,128)(2,1)S(1)} %copy-done, bf16[16,2,256,256]{3,2,1,0:T(8,128)(2,1)} %collective-permute-done.16.theirs), custom_call_target="tpu_custom_call" | custom-call | flops 2147483648 | bytes 16777216 | tf_op jit(solution)/shard_map/output/pallas_call | solution.py:293
  142.5 16.3 %all-to-all-done.got = bf16[32,48,512]{2,1,0:T(8,128)(2,1)S(1)} async-done(((bf16[32,48,512]{2,1,0:T(8,128)(2,1)}), bf16[32,48,512]{2,1,0:T(8,128)(2,1)S(1)}, u32[]{:S(2)}, u32[]{:S(2)}) %all-to-all-start) | async-done | bytes 1572896 | tf_op jit(solution)/shard_map/all_to_all | solution.py:422
  158.8 1.2 total.1
  (27 shorter events, 0.2 us)
Async XLA Ops:
  1.4 1.0 copy-start.1
  2.4 0.9 copy-start.2
  3.3 0.9 copy-start.3
  4.2 0.9 copy-start.4
  5.1 0.8 copy-start.5
  6.6 17.3 %collective-permute-start = (bf16[896,256]{1,0:T(8,128)(2,1)S(1)}, bf16[896,256]{1,0:T(8,128)(2,1)S(1)}, u32[]{:S(2)}, u32[]{:S(2)}) collective-permute-start(bf16[896,256]{1,0:T(8,128)(2,1)S(1)} %pack.1), channel_id=1, source_target_pairs={{0,4},{4,0},{8,12},{12,8},{16,20},{20,16},{24,28},{28,24},{32,36},... | collective-permute-start | bytes 1376264 | tf_op jit(solution)/shard_map/ppermute | solution.py:379
  8.8 15.1 %collective-permute-start.1 = (bf16[896,256]{1,0:T(8,128)(2,1)S(1)}, bf16[896,256]{1,0:T(8,128)(2,1)S(1)}, u32[]{:S(2)}, u32[]{:S(2)}) collective-permute-start(bf16[896,256]{1,0:T(8,128)(2,1)S(1)} %pack.1), channel_id=1, source_target_pairs={{0,8},{1,33},{2,10},{3,35},{4,12},{5,37},{6,14},{7,39},{8,16},{9,4... | collective-permute-start | bytes 1376264 | tf_op jit(solution)/shard_map/ppermute | solution.py:371
  10.7 15.0 %collective-permute-start.2 = (bf16[896,256]{1,0:T(8,128)(2,1)S(1)}, bf16[896,256]{1,0:T(8,128)(2,1)S(1)}, u32[]{:S(2)}, u32[]{:S(2)}) collective-permute-start(bf16[896,256]{1,0:T(8,128)(2,1)S(1)} %pack.1), channel_id=1, source_target_pairs={{0,16},{1,65},{2,18},{3,67},{4,20},{5,69},{6,22},{7,71},{8,24},{9,... | collective-permute-start | bytes 1376264 | tf_op jit(solution)/shard_map/ppermute | solution.py:371
  14.3 11.4 %collective-permute-start.3 = (bf16[896,256]{1,0:T(8,128)(2,1)S(1)}, bf16[896,256]{1,0:T(8,128)(2,1)S(1)}, u32[]{:S(2)}, u32[]{:S(2)}) collective-permute-start(bf16[896,256]{1,0:T(8,128)(2,1)S(1)} %pack.1), channel_id=1, source_target_pairs={{0,24},{1,97},{2,26},{3,99},{4,28},{5,101},{6,30},{7,103},{8,0},{9... | collective-permute-start | bytes 1376264 | tf_op jit(solution)/shard_map/ppermute | solution.py:371
  25.6 21.0 %collective-permute-start.4 = (bf16[256,8192]{1,0:T(8,128)(2,1)S(1)}, bf16[256,8192]{1,0:T(8,128)(2,1)S(1)}, u32[]{:S(2)}, u32[]{:S(2)}) collective-permute-start(bf16[256,8192]{1,0:T(8,128)(2,1)S(1)} %get-tuple-element.44), channel_id=1, source_target_pairs={{0,1},{1,0},{2,3},{3,2},{4,5},{5,4},{6,7},{7,6},{8,9},{9,8},{10,11... | collective-permute-start | bytes 12582920 | tf_op jit(solution)/shard_map/ppermute | solution.py:374
  25.6 22.9 %collective-permute-start.5 = (bf16[256,8192]{1,0:T(8,128)(2,1)}, bf16[256,8192]{1,0:T(8,128)(2,1)}, u32[]{:S(2)}, u32[]{:S(2)}) collective-permute-start(bf16[256,8192]{1,0:T(8,128)(2,1)} %get-tuple-element.45), channel_id=1, source_target_pairs={{0,1},{1,0},{2,3},{3,2},{4,5},{5,4},{6,7},{7,6},{8,9},{9,8},{10,11... | collective-permute-start | bytes 12582920 | tf_op jit(solution)/shard_map/ppermute | solution.py:374
  26.1 13.0 %collective-permute-start.8 = (bf16[896,256]{1,0:T(8,128)(2,1)S(1)}, bf16[896,256]{1,0:T(8,128)(2,1)S(1)}, u32[]{:S(2)}, u32[]{:S(2)}) collective-permute-start(bf16[896,256]{1,0:T(8,128)(2,1)S(1)} %collective-permute-done), channel_id=1, source_target_pairs={{0,24},{1,97},{2,26},{3,99},{4,28},{5,101},{6,30},{7,103},{8,0},{9... | collective-permute-start | bytes 1376264 | tf_op jit(solution)/shard_map/ppermute | solution.py:371
  28.2 11.0 %collective-permute-start.9 = (bf16[896,256]{1,0:T(8,128)(2,1)S(1)}, bf16[896,256]{1,0:T(8,128)(2,1)S(1)}, u32[]{:S(2)}, u32[]{:S(2)}) collective-permute-start(bf16[896,256]{1,0:T(8,128)(2,1)S(1)} %collective-permute-done), channel_id=1, source_target_pairs={{0,16},{1,65},{2,18},{3,67},{4,20},{5,69},{6,22},{7,71},{8,24},{9,... | collective-permute-start | bytes 1376264 | tf_op jit(solution)/shard_map/ppermute | solution.py:371
  29.6 13.5 %collective-permute-start.6 = (bf16[896,256]{1,0:T(8,128)(2,1)S(1)}, bf16[896,256]{1,0:T(8,128)(2,1)S(1)}, u32[]{:S(2)}, u32[]{:S(2)}) collective-permute-start(bf16[896,256]{1,0:T(8,128)(2,1)S(1)} %collective-permute-done), channel_id=1, source_target_pairs={{0,8},{1,33},{2,10},{3,35},{4,12},{5,37},{6,14},{7,39},{8,16},{9,4... | collective-permute-start | bytes 1376264 | tf_op jit(solution)/shard_map/ppermute | solution.py:371
  39.5 23.8 %collective-permute-start.10 = (bf16[2,2,896,256]{3,2,1,0:T(8,128)(2,1)S(1)}, bf16[2,2,896,256]{3,2,1,0:T(8,128)(2,1)S(1)}, u32[]{:S(2)}, u32[]{:S(2)}) collective-permute-start(bf16[2,2,896,256]{3,2,1,0:T(8,128)(2,1)S(1)} %pad_maximum_fusion.1.far), channel_id=1, source_target_pairs={{0,96},{1,25},{2,98},{3,27},{4,100},{5,29},{6,102},{7,31},{8,104},... | collective-permute-start | bytes 5505032 | tf_op jit(solution)/shard_map/ppermute | solution.py:371
  43.4 24.5 %collective-permute-start.7 = (bf16[2,2,896,256]{3,2,1,0:T(8,128)(2,1)S(1)}, bf16[2,2,896,256]{3,2,1,0:T(8,128)(2,1)S(1)}, u32[]{:S(2)}, u32[]{:S(2)}) collective-permute-start(bf16[2,2,896,256]{3,2,1,0:T(8,128)(2,1)S(1)} %pad_maximum_fusion.near), channel_id=1, source_target_pairs={{0,32},{1,9},{2,34},{3,11},{4,36},{5,13},{6,38},{7,15},{8,40},{9,1... | collective-permute-start | bytes 5505032 | tf_op jit(solution)/shard_map/ppermute | solution.py:371
  45.0 42.5 %collective-permute-start.13 = (bf16[2,2,896,256]{3,2,1,0:T(8,128)(2,1)S(1)}, bf16[2,2,896,256]{3,2,1,0:T(8,128)(2,1)S(1)}, u32[]{:S(2)}, u32[]{:S(2)}) collective-permute-start(bf16[2,2,896,256]{3,2,1,0:T(8,128)(2,1)S(1)} %pad_maximum_fusion.1.far), channel_id=1, source_target_pairs={{0,32},{1,9},{2,34},{3,11},{4,36},{5,13},{6,38},{7,15},{8,40},{9,1... | collective-permute-start | bytes 5505032 | tf_op jit(solution)/shard_map/ppermute | solution.py:371
  46.6 2.0 %copy-start.6 = (bf16[256,8192]{1,0:T(8,128)(2,1)}, bf16[256,8192]{1,0:T(8,128)(2,1)S(1)}, u32[]{:S(2)}) copy-start(bf16[256,8192]{1,0:T(8,128)(2,1)S(1)} %collective-permute-done.4.mate_tok) | copy-start | bytes 12582916
  46.6 40.9 %collective-permute-start.14 = (bf16[2,2,896,256]{3,2,1,0:T(8,128)(2,1)S(1)}, bf16[2,2,896,256]{3,2,1,0:T(8,128)(2,1)}, u32[]{:S(2)}, u32[]{:S(2)}) collective-permute-start(bf16[2,2,896,256]{3,2,1,0:T(8,128)(2,1)S(1)} %pad_maximum_fusion.near), channel_id=1, source_target_pairs={{0,96},{1,25},{2,98},{3,27},{4,100},{5,29},{6,102},{7,31},{8,104},... | collective-permute-start | bytes 5505032 | tf_op jit(solution)/shard_map/ppermute | solution.py:371
  63.4 7.8 %copy-start.7 = (bf16[2,2,896,256]{3,2,1,0:T(8,128)(2,1)}, bf16[2,2,896,256]{3,2,1,0:T(8,128)(2,1)S(1)}, u32[]{:S(2)}) copy-start(bf16[2,2,896,256]{3,2,1,0:T(8,128)(2,1)S(1)} %collective-permute-done.10.far) | copy-start | bytes 5505028
  67.9 39.3 %collective-permute-start.11 = (bf16[2,2,896,256]{3,2,1,0:T(8,128)(2,1)S(1)}, bf16[2,2,896,256]{3,2,1,0:T(8,128)(2,1)S(1)}, u32[]{:S(2)}, u32[]{:S(2)}) collective-permute-start(bf16[2,2,896,256]{3,2,1,0:T(8,128)(2,1)S(1)} %collective-permute-done.7.near), channel_id=1, source_target_pairs={{0,32},{1,9},{2,34},{3,11},{4,36},{5,13},{6,38},{7,15},{8,40},{9,1... | collective-permute-start | bytes 5505032 | tf_op jit(solution)/shard_map/ppermute | solution.py:371
  68.2 39.0 %collective-permute-start.12 = (bf16[2,2,896,256]{3,2,1,0:T(8,128)(2,1)S(1)}, bf16[2,2,896,256]{3,2,1,0:T(8,128)(2,1)}, u32[]{:S(2)}, u32[]{:S(2)}) collective-permute-start(bf16[2,2,896,256]{3,2,1,0:T(8,128)(2,1)S(1)} %collective-permute-done.10.far), channel_id=1, source_target_pairs={{0,96},{1,25},{2,98},{3,27},{4,100},{5,29},{6,102},{7,31},{8,104},... | collective-permute-start | bytes 5505032 | tf_op jit(solution)/shard_map/ppermute | solution.py:371
  107.2 10.4 %copy-start.8 = (bf16[2,16,384]{2,1,0:T(8,128)(2,1)S(1)}, bf16[2,16,384]{2,1,0:T(8,128)(2,1)}, u32[]{:S(2)}) copy-start(bf16[2,16,384]{2,1,0:T(8,128)(2,1)} %param.17) | copy-start | bytes 73732
  114.5 2.3 %collective-permute-start.15 = (f32[256,768]{1,0:T(8,128)S(1)}, f32[256,768]{1,0:T(8,128)S(1)}, u32[]{:S(2)}, u32[]{:S(2)}) collective-permute-start(f32[256,768]{1,0:T(8,128)S(1)} %get-tuple-element.69), channel_id=1, source_target_pairs={{0,1},{1,0},{2,3},{3,2},{4,5},{5,4},{6,7},{7,6},{8,9},{9,8},{10,11... | collective-permute-start | bytes 2359304 | tf_op jit(solution)/shard_map/ppermute | solution.py:374
  116.8 14.2 %collective-permute-start.16 = (bf16[16,2,256,256]{3,2,1,0:T(8,128)(2,1)}, bf16[16,2,256,256]{3,2,1,0:T(8,128)(2,1)}, u32[]{:S(2)}, u32[]{:S(2)}) collective-permute-start(bf16[16,2,256,256]{3,2,1,0:T(8,128)(2,1)} %get-tuple-element.76.own), channel_id=1, source_target_pairs={{0,1},{1,0},{2,3},{3,2},{4,5},{5,4},{6,7},{7,6},{8,9},{9,8},{10,11... | collective-permute-start | bytes 12582920 | tf_op jit(solution)/shard_map/ppermute | solution.py:374
  125.3 33.5 %all-to-all-start = ((bf16[32,48,512]{2,1,0:T(8,128)(2,1)}), bf16[32,48,512]{2,1,0:T(8,128)(2,1)S(1)}, u32[]{:S(2)}, u32[]{:S(2)}) async-start(bf16[32,48,512]{2,1,0:T(8,128)(2,1)} %term.1), calls=%async_computation | async-start | bytes 3145728 | tf_op jit(solution)/shard_map/all_to_all | solution.py:422
  131.0 2.2 %copy-start = (bf16[16,2,256,256]{3,2,1,0:T(8,128)(2,1)S(1)}, bf16[16,2,256,256]{3,2,1,0:T(8,128)(2,1)}, u32[]{:S(2)}) copy-start(bf16[16,2,256,256]{3,2,1,0:T(8,128)(2,1)} %get-tuple-element.76.own) | copy-start | bytes 12582916

commit v3 on v2

--- a/solution.py
+++ b/solution.py
@@ -54,141 +54,112 @@
             out_specs=pl.BlockSpec((3 * half + 2 * low, half), lambda k, w: (0, 0)),
         ),
         out_shape=jax.ShapeDtypeStruct((3 * half + 2 * low, half), BF16),
-        compiler_params=params(),
+        compiler_params=pltpu.CompilerParams(vmem_limit_bytes=56 * 1024 * 1024),
         name="pack",
     )(where, w_query, w_key, w_value, down, w_output)
 
 
-def pick_kernel(where, a, b, out_a, out_b):
-    piece = 256
-    for side in range(2):
-
-        @pl.when(where[0] == side)
+def arrive_kernel(where, *refs, pieces, fresh):
+    tok, cot, mate_tok, mate_cot = refs[0:2], refs[2:4], refs[4:6], refs[6:8]
+    arrived, refs = refs[8 : 8 + pieces], refs[8 + pieces :]
+    both, low, kept = refs[-3:]
+    step = pl.program_id(0)
+
+    if fresh:
+
+        @pl.when(step == 0)
         def _():
-            for full, out in ((a, out_a), (b, out_b)):
-                for i in range(out.shape[1] // piece):
-                    at = (2 * i + 1 - side) * piece
-                    out[:, i * piece : (i + 1) * piece] = full[:, at : at + piece]
-
-
-def pick(a, b, where):
-    seq, width = a.shape
-    block = 4096
-    return pl.pallas_call(
-        pick_kernel,
+            for new in (both, low):
+                new[...] = jnp.zeros_like(new)
+
+    core, slot = where[0], where[1]
+    half = arrived[0].shape[2]
+    first = arrived[0].shape[1] - half
+
+    def add(shard):
+        side = pl.multiple_of(core * half, half)
+        rows = jnp.concatenate(
+            [
+                jnp.concatenate([t[:, pl.ds(side, half)] for t in tok], axis=1),
+                jnp.concatenate([t[...] for t in mate_tok], axis=1),
+            ],
+            axis=0,
+        )
+        for g in range(2):
+            cols = slice(g * half, (g + 1) * half)
+            both[:, cols] += dot(rows, jnp.concatenate([shard[i, cols, :] for i in range(2)], axis=0))
+        rows = jnp.concatenate([jnp.concatenate([t[...] for t in two], axis=1) for two in (cot, mate_cot)], axis=0)
+        w = jnp.concatenate([shard[i, first:, :] for i in range(2)], axis=1)
+        both[:, 2 * half :] += dot(rows, w, NT)
+        kept[...] = shard[:, first:, :]
+        down = [
+            shard[i, pl.ds(pl.multiple_of(2 * half + h * 64 + slot * 32, 32), 32), :]
+            for i in range(2)
+            for h in range(2)
+        ]
+        rows = jnp.concatenate([t[...] for t in tok], axis=1)
+        low[...] += dot(rows, jnp.concatenate(down, axis=1), NT)
+
+    for i in range(pieces):
+
+        @pl.when(step == i)
+        def _():
+            add(arrived[i])
+
+
+def place(w, early, late):
+    y = (w[3] - jnp.where(w[0] == 0, late, early) + Y) % Y
+    z = (w[4] - jnp.where(w[0] == 0, early, late) + Z) % Z
+    return y * Z + z
+
+
+def arrive(where, tokens, cotangent, mate_tok, mate_cot, pieces, lates, flip, base, sums, out_shape):
+    seq = tokens.shape[0]
+    rows, half = pieces[0][0].shape[1:]
+
+    def at(k, w, p):
+        late = jnp.where(k < 2, lates[0], lates[-1])
+        return 2 * place(w, 2 * (k % 2) + p, late) + (w[2] ^ flip)
+
+    def two(cols, index):
+        return [pl.BlockSpec((seq, cols), lambda k, w, p=p: (0, index(k, w, p))) for p in range(2)]
+
+    core_half = lambda k, w, p: 2 * at(k, w, p) + w[0]
+    whole = [pl.BlockSpec(memory_space=pltpu.VMEM)] * 2
+    fresh = [x is None for x in sums]
+    given = [x for x in sums if x is not None]
+    inputs = [tokens] * 2 + [cotangent] * 2 + [mate_tok] * 2 + [mate_cot] * 2 + [a for a, _ in pieces]
+    kept_at = [i for i in range(3) if not fresh[i]]
+    kept_spec = [] if fresh[2] else [pl.BlockSpec(memory_space=pl.ANY)]
+    return pl.pallas_call(
+        functools.partial(arrive_kernel, pieces=len(pieces), fresh=fresh[0]),
         grid_spec=pltpu.PrefetchScalarGridSpec(
             num_scalar_prefetch=1,
-            grid=(width // block,),
-            in_specs=[pl.BlockSpec((seq, block), lambda k, w: (0, k))] * 2,
-            out_specs=[pl.BlockSpec((seq, block // 2), lambda k, w: (0, k))] * 2,
-        ),
-        out_shape=[jax.ShapeDtypeStruct((seq, width // 2), BF16)] * 2,
-        compiler_params=params(),
-        cost_estimate=pl.CostEstimate(flops=0, bytes_accessed=6 * seq * width, transcendentals=0),
-        name="pick",
-    )(where, a, b)
-
-
-def arrive_kernel(where, tok, cot_a, cot_b, mate_tok, mate_cot, near, far, *refs, fresh):
-    *after, kept = refs[-4:]
-    step = pl.program_id(0)
-
-    @pl.when(step == 0)
-    def _():
-        for i, new in enumerate(after):
-            new[...] = jnp.zeros_like(new) if fresh else refs[i][...]
-
-    mine, other, low = after
-    core, slot, x_hi = where[0], where[1], where[2]
-    half = near.shape[3]
-    first = near.shape[2] - half
-
-    def add(pair):
-        own = jnp.concatenate(
-            [tok[:, pl.ds(pl.multiple_of((2 * x + core) * half, half), half)] for x in range(2)], axis=1
-        )
-        at = [x ^ x_hi for x in range(2)]
-        for g in range(2):
-            cols = slice(g * half, (g + 1) * half)
-            w = jnp.concatenate([pair[0, i, cols, :] for i in at], axis=0)
-            mine[:, cols] += dot(own, w)
-            other[:, cols] += dot(mate_tok[...], w)
-        w = [pair[0, i, first:, :] for i in at]
-        cols = slice(2 * half, 3 * half)
-        both = jnp.concatenate(w, axis=1)
-        mine[:, cols] += dot(jnp.concatenate([cot_a[...], cot_b[...]], axis=1), both, NT)
-        other[:, cols] += dot(mate_cot[...], both, NT)
-        for x in range(2):
-            kept[0, x] = w[x]
-        down = [
-            pair[0, i, pl.ds(pl.multiple_of(2 * half + h * 64 + slot * 32, 32), 32), :]
-            for i in at
-            for h in range(2)
-        ]
-        low[...] += dot(tok[...], jnp.concatenate(down, axis=1), NT)
-
-    count = pl.num_programs(0) // 2
-
-    @pl.when(step < count)
-    def _():
-        add(near)
-
-    @pl.when(step >= count)
-    def _():
-        add(far)
-
-
-def arrive(where, tokens, cotangent, mate_tok, mate_cot, first, second, sums, out_shape):
-    seq = tokens.shape[0]
-    count, _, rows, half = first[0].shape
-    steps = first[1] + second[1]
-
-    def at(k, w):
-        early = jnp.int32(steps[0])
-        for i in range(1, len(steps)):
-            early = jnp.where(k == i, steps[i], early)
-        late = jnp.where(k < count, first[2], second[2])
-        y = (w[3] - jnp.where(w[0] == 0, late, early) + Y) % Y
-        z = (w[4] - jnp.where(w[0] == 0, early, late) + Z) % Z
-        return y * Z + z
-
-    whole = [pl.BlockSpec(x.shape, lambda k, w: (0, 0)) for x in out_shape[:3]]
-    block = (1, 2, rows, half)
-    fresh = not sums
-    return pl.pallas_call(
-        functools.partial(arrive_kernel, fresh=fresh),
-        grid_spec=pltpu.PrefetchScalarGridSpec(
-            num_scalar_prefetch=1,
-            grid=(2 * count,),
-            in_specs=[
-                pl.BlockSpec((seq, 4 * half), lambda k, w: (0, at(k, w))),
-                pl.BlockSpec((seq, half), lambda k, w: (0, 4 * at(k, w) + w[0])),
-                pl.BlockSpec((seq, half), lambda k, w: (0, 4 * at(k, w) + 2 + w[0])),
-                pl.BlockSpec((seq, 2 * half), lambda k, w: (0, at(k, w))),
-                pl.BlockSpec((seq, 2 * half), lambda k, w: (0, at(k, w))),
-                pl.BlockSpec(block, lambda k, w: (jnp.minimum(k, count - 1), 0, 0, 0)),
-                pl.BlockSpec(block, lambda k, w: (jnp.maximum(k - count, 0), 0, 0, 0)),
-            ]
-            + ([] if fresh else whole + [pl.BlockSpec(memory_space=pl.ANY)]),
-            out_specs=whole + [pl.BlockSpec((1, 2, half, half), lambda k, w: (at(k, w), 0, 0, 0))],
+            grid=(len(pieces),),
+            in_specs=two(2 * half, at)
+            + two(half, core_half) * 3
+            + [pl.BlockSpec((2, rows, half), lambda k, w, i=i: (i, 0, 0)) for _, i in pieces]
+            + ([] if fresh[0] else whole)
+            + kept_spec,
+            out_specs=whole + [pl.BlockSpec((2, half, half), lambda k, w: (base + k, 0, 0))],
         ),
         out_shape=out_shape,
-        input_output_aliases={} if fresh else {11: 3},
+        input_output_aliases=dict(zip(range(1 + len(inputs), 1 + len(inputs) + len(given)), kept_at)),
         compiler_params=params(),
-        cost_estimate=pl.CostEstimate(flops=count * 2**30, bytes_accessed=count * 2**22, transcendentals=0),
+        cost_estimate=pl.CostEstimate(flops=len(pieces) * 2**29, bytes_accessed=len(pieces) * 2**21, transcendentals=0),
         name="arrive",
-    )(where, tokens, cotangent, cotangent, mate_tok, mate_cot, first[0], second[0], *sums)
+    )(where, *inputs, *given)
 
 
 def attend_kernel(head, scalars, mine, other, low_in, up, context, mid, up_sum):
-    seq, total = mine.shape
+    seq, total = other.shape
     q_cols = (total - 2 * head) // 2
     heads = q_cols // head
     length = scalars[1]
     inv_root = 1.0 / jnp.sqrt(F32(head))
     low = low_in[...].astype(BF16)
     added = ADAPTER_SCALE * dot(low, up[...])
-    summed = mine[...] + other[...]
+    summed = mine[:seq, :] + other[...]
     qkv, dctx = summed[:, : total - q_cols], summed[:, total - q_cols :]
     query = (qkv[:, :q_cols] + added[:, :q_cols]).astype(BF16)
     key = qkv[:, q_cols : q_cols + head].astype(BF16)
@@ -225,7 +196,7 @@
 
 
 def attend(scalars, mine, other, low, up, head):
-    seq, total = mine.shape
+    seq, total = other.shape
     q_cols = (total - 2 * head) // 2
     vmem = pl.BlockSpec(memory_space=pltpu.VMEM)
     rank2 = low.shape[1]
@@ -271,38 +242,47 @@
     )(mid, up_sum, tokens)
 
 
-def output_kernel(where, context, own, theirs, out):
-    pairs, _, rows, half = own.shape
+def output_kernel(where, context, own, flipped, their_own, their_flipped, out):
+    half = own.shape[1]
     for core in range(2):
-
-        @pl.when(where[0] == core)
-        def _():
-            halves = (own, theirs) if core == 0 else (theirs, own)
-            for p in range(pairs):
+        for x_hi in range(2):
+
+            @pl.when((where[0] == core) & (where[2] == x_hi))
+            def _():
+                shards = [(own, their_own), (flipped, their_flipped)]
                 for x in range(2):
-                    w = jnp.concatenate([h[p, x] for h in halves], axis=1)
-                    at = (2 * p + x) * 2 * half
-                    out[:, at : at + 2 * half] = dot(context[...], w).astype(BF16)
-
-
-def output_of(where, context, own, theirs, cost):
+                    mine, theirs = shards[x ^ x_hi]
+                    two = (mine, theirs) if core == 0 else (theirs, mine)
+                    w = jnp.concatenate([h[0] for h in two], axis=1)
+                    out[:, 2 * x * half : 2 * (x + 1) * half] = dot(context[...], w).astype(BF16)
+
+
+def output_of(where, context, own, flipped, their_own, their_flipped, cost):
     seq, cols = context.shape
-    count, _, rows, half = own.shape
-    per = 2
-    weights = pl.BlockSpec((per, 2, rows, half), lambda k, w: (k, 0, 0, 0))
+    count, rows, half = own.shape
+
+    def late_of(k):
+        return jnp.where(k < 8, k // 4, 5 - k // 4)
+
+    def partner(k):
+        early, late = k % 4, late_of(k)
+        return jnp.where(early < 2, early, 5 - early) * 4 + late
+
+    mine = pl.BlockSpec((1, rows, half), lambda k, w: (k, 0, 0))
+    theirs = pl.BlockSpec((1, rows, half), lambda k, w: (partner(k), 0, 0))
     return pl.pallas_call(
         output_kernel,
         grid_spec=pltpu.PrefetchScalarGridSpec(
             num_scalar_prefetch=1,
-            grid=(count // per,),
-            in_specs=[pl.BlockSpec((seq, cols), lambda k, w: (0, 0)), weights, weights],
-            out_specs=pl.BlockSpec((seq, per * 4 * half), lambda k, w: (0, k)),
+            grid=(count,),
+            in_specs=[pl.BlockSpec((seq, cols), lambda k, w: (0, 0)), mine, mine, theirs, theirs],
+            out_specs=pl.BlockSpec((seq, 4 * half), lambda k, w: (0, place(w, k % 4, late_of(k)))),
         ),
         out_shape=jax.ShapeDtypeStruct((seq, count * 4 * half), BF16),
         compiler_params=params(),
         cost_estimate=cost,
         name="output",
-    )(where, context, own, theirs)
+    )(where, context, own, flipped, their_own, their_flipped)
 
 
 def total_kernel(got, down, up):
@@ -379,37 +359,47 @@
     flipped = lax.ppermute(piece, "fsdp", [(f, f ^ 1) for f in range(parts)])
     hops = (1, 3, 2)
     early = {j: shift(piece, j, False) for j in hops}
-    halves = pick(tokens, cotangent, where)
-    flipped, early, halves = lax.optimization_barrier((flipped, early, halves))
+    mate_tok = swap(tokens)
+    flipped, early, mate_tok = lax.optimization_barrier((flipped, early, mate_tok))
+    early[0] = piece
+    own = jnp.stack([early[j] for j in range(4)])
+    own_ahead, own_behind = shift(own, 1, True), shift(own, -1, True)
     early_flipped = {j: shift(flipped, j, False) for j in hops}
-    mate_tok, mate_cot = (swap(half) for half in halves)
-    early[0], early_flipped[0] = piece, flipped
-
-    def group(steps):
-        return jnp.stack([jnp.stack([early[j], early_flipped[j]]) for j in steps])
-
-    near, far = (0, 1), (3, 2)
-    here_near, here_far = group(near), group(far)
-    ahead_near, behind_far = shift(here_near, 1, True), shift(here_far, -1, True)
-    ahead_far, behind_near = shift(here_far, 1, True), shift(here_near, -1, True)
-    out_shape = [jax.ShapeDtypeStruct((seq, 2 * (q_cols + head)), F32)] * 2 + [
+    early_flipped, own_ahead, own_behind, cot_then = lax.optimization_barrier(
+        (early_flipped, own_ahead, own_behind, cotangent)
+    )
+    mate_cot = swap(cot_then)
+    early_flipped[0] = flipped
+    flip = jnp.stack([early_flipped[j] for j in range(4)])
+    flip_ahead, flip_behind = shift(flip, 1, True), shift(flip, -1, True)
+    kept_shape = jax.ShapeDtypeStruct((parts // 2, q_cols, shard // 2), BF16)
+    out_shape = [
+        jax.ShapeDtypeStruct((2 * seq, 2 * (q_cols + head)), F32),
         jax.ShapeDtypeStruct((seq, 2 * rank), F32),
-        jax.ShapeDtypeStruct((parts // 2, 2, q_cols, shard // 2), BF16),
+        kept_shape,
     ]
 
-    def add(first, second, sums):
-        return arrive(where, tokens, cotangent, mate_tok, mate_cot, first, second, sums, out_shape)
-
-    sums = add((here_near, near, 0), (here_far, far, 0), ())
-    ahead_near, behind_far, sums = lax.optimization_barrier((ahead_near, behind_far, sums))
-    far_ahead, far_behind = shift(ahead_near, 1, True), shift(behind_far, -1, True)
-    sums = add((ahead_near, near, 1), (behind_far, far, 3), sums)
-    sums = add((ahead_far, far, 1), (behind_near, near, 3), sums)
-    sums = add((far_ahead, near, 2), (far_behind, far, 2), sums)
-    summed, other, low, kept = sums
-    other = swap(other)
-    other, kept = lax.optimization_barrier((other, kept))
-    theirs = swap(kept)
+    def add(pieces, lates, flip, base, sums):
+        return arrive(
+            where, tokens, cotangent, mate_tok, mate_cot, pieces, lates, flip, base, sums, out_shape
+        )
+
+    def halves(array):
+        return [(array, 0), (array, 1)]
+
+    *sums, kept = add(halves(own), (0,), 0, 0, (None, None, None))
+    own_far = shift(own_ahead[:2], 1, True), shift(own_behind[2:], -1, True)
+    *sums, kept = add(halves(own_ahead) + halves(own_behind), (1, 3), 0, 2, (*sums, kept))
+    *sums, kept_flip = add(halves(flip), (0,), 1, 0, (*sums, None))
+    flip_ahead, flip_behind, sums = lax.optimization_barrier((flip_ahead, flip_behind, sums))
+    flip_far = shift(flip_ahead[:2], 1, True), shift(flip_behind[2:], -1, True)
+    *sums, kept_flip = add(halves(flip_ahead) + halves(flip_behind), (1, 3), 1, 2, (*sums, kept_flip))
+    *sums, kept = add([(x, 0) for x in own_far], (2,), 0, 6, (*sums, kept))
+    *sums, kept_flip = add([(x, 0) for x in flip_far], (2,), 1, 6, (*sums, kept_flip))
+    summed, low = sums
+    other = swap(summed[seq:])
+    other, kept, kept_flip = lax.optimization_barrier((other, kept, kept_flip))
+    theirs, their_flip = swap(kept), swap(kept_flip)
 
     up = lax.dynamic_index_in_dim(adapter_up, slot, 0, keepdims=False)
     at_query = jnp.arange(q_cols + head)[None, :] < q_cols
@@ -423,7 +413,7 @@
     cost = pl.CostEstimate(
         flops=2 * seq * q_cols * width, bytes_accessed=4 * seq * width, transcendentals=0
     )
-    output = output_of(where, context, kept, theirs, cost)
+    output = output_of(where, context, kept, kept_flip, theirs, their_flip, cost)
     got, output = lax.optimization_barrier((got, output))
     down_sum, grad_up = total(got, 2 * rank, q_cols + head)
     grad_down = down_sum.reshape(slots * 2 * rank, shard).T.reshape(shard, slots, 2, rank)

time: 161 us -> 158 us (0.981)
  waiting for transfers between devices: 64.1 us -> 57.2 us
  starting transfers between devices: 30.2 us -> 34.2 us
  local copies, waits for them, and re-layouts: 7.13 us -> 4.24 us
  Pallas kernels: 55.7 us -> 57.7 us
    ppermute x12 -> x14, waiting for transfers between devices: 45.5 us -> 30.9 us  [shift(): return lax.ppermute(array, ('fsdp', 'tenant'), to)]
    ppermute x4 -> x5, waiting for transfers between devices: 2.29 us -> 8.73 us  [swap(): return lax.ppermute(array, 'tenant', [(t, t ^ 1) for t in range(tenants)])]
    ppermute x1, waiting for transfers between devices: 0.01 us -> 5.97 us  [body(): flipped = lax.ppermute(piece, 'fsdp', [(f, f ^ 1) for f in range(parts)])]
    pallas_call x1, Pallas kernels: 9.3 us -> 14.7 us  [output_of(): pl.pallas_call(output_kernel, grid_spec=pltpu.PrefetchScalarGridSpec(num_...]
    pallas_call x5 -> x6, Pallas kernels: 37 us -> 31.6 us  [arrive(): pl.pallas_call(functools.partial(arrive_kernel, pieces=len(pieces), fresh...]
    unnamed x18 -> x8, local copies, waits for them, and re-layouts: 7.04 us -> 2.11 us
    all_to_all x1, waiting for transfers between devices: 16.3 us -> 11.6 us  [body(): got = lax.all_to_all(sent, 'fsdp', split_axis=0, concat_axis=0, tiled=True)]
    ppermute x12 -> x14, starting transfers between devices: 21.6 us -> 25.2 us  [shift(): return lax.ppermute(array, ('fsdp', 'tenant'), to)]
  transfers between devices with their start and end apart: 18 -> 21, of which waited for: 9 -> 10; matrix products, arithmetic and copies ran while one was open for 0% -> 2% of each run, Pallas kernels for 29% -> 33%
where the time goes in v3:
time: 158 us; the launch traced here: 157 us
  Pallas kernels  57.7 us (37%)
  waiting for transfers between devices  57.2 us (36%)
  starting transfers between devices  34.2 us (22%)
  local copies, waits for them, and re-layouts  4.24 us (3%)
  between operations  2.15 us (1%)
  other arithmetic  1.58 us (1%)
    pallas_call x6, Pallas kernels, arrive(): pl.pallas_call(functools.partial(arrive_kernel, pieces=len(pieces), fresh...  31.6 us
    ppermute x14, waiting for transfers between devices, shift(): return lax.ppermute(array, ('fsdp', 'tenant'), to)  30.9 us
    ppermute x14, starting transfers between devices, shift(): return lax.ppermute(array, ('fsdp', 'tenant'), to)  25.2 us
    pallas_call x1, Pallas kernels, output_of(): pl.pallas_call(output_kernel, grid_spec=pltpu.PrefetchScalarGridSpec(num_...  14.7 us
    all_to_all x1, waiting for transfers between devices, body(): got = lax.all_to_all(sent, 'fsdp', split_axis=0, concat_axis=0, tiled=True)  11.6 us
    ppermute x5, waiting for transfers between devices, swap(): return lax.ppermute(array, 'tenant', [(t, t ^ 1) for t in range(tenants)])  8.73 us
    all_to_all x1, starting transfers between devices, body(): got = lax.all_to_all(sent, 'fsdp', split_axis=0, concat_axis=0, tiled=True)  6.15 us
    ppermute x1, waiting for transfers between devices, body(): flipped = lax.ppermute(piece, 'fsdp', [(f, f ^ 1) for f in range(parts)])  5.97 us
  transfers between devices with their start and end apart: 21, of which 10 were waited for; matrix products, arithmetic and copies ran while one was open for 2% of the time, Pallas kernels for 33%

profile of v3, /device:TPU:2, one launch (start us, length us, event | category | flops | bytes accessed | tf_op | source)
XLA Modules:
  0.0 157.1 jit_solution(7002583798929337518)
XLA Ops:
  0.6 0.1 collective-permute-start.4
  1.4 0.7 stack.53.where
  2.1 2.5 %pack.1 = bf16[896,256]{1,0:T(8,128)(2,1)} custom-call(s32[5]{0:T(128)} %stack.53.where, bf16[512,256]{1,0:T(8,128)(2,1)} %w_query.1, bf16[512,128]{1,0:T(8,128)(2,1)} %w_key.1, bf16[512,128]{1,0:T(8,128)(2,1)} %w_value.1, bf16[64,512]{1,0:T(8,128)(2,1)} %bitcast.35, bf16[256,512]{1,0:T(8,128)(2,1)} %w_output.1), custom_call_target="tpu_custom_call" | custom-call | tf_op jit(solution)/shard_map/pack/pallas_call | solution.py:42
  4.6 2.1 %collective-permute-start = (bf16[896,256]{1,0:T(8,128)(2,1)}, bf16[896,256]{1,0:T(8,128)(2,1)S(1)}, u32[]{:S(2)}, u32[]{:S(2)}) collective-permute-start(bf16[896,256]{1,0:T(8,128)(2,1)} %pack.1), channel_id=1, source_target_pairs={{0,4},{4,0},{8,12},{12,8},{16,20},{20,16},{24,28},{28,24},{32,36},... | collective-permute-start | bytes 1376264 | tf_op jit(solution)/shard_map/ppermute | solution.py:359
  6.8 1.9 %collective-permute-start.1 = (bf16[896,256]{1,0:T(8,128)(2,1)}, bf16[896,256]{1,0:T(8,128)(2,1)S(1)}, u32[]{:S(2)}, u32[]{:S(2)}) collective-permute-start(bf16[896,256]{1,0:T(8,128)(2,1)} %pack.1), channel_id=1, source_target_pairs={{0,8},{1,33},{2,10},{3,35},{4,12},{5,37},{6,14},{7,39},{8,16},{9,4... | collective-permute-start | bytes 1376264 | tf_op jit(solution)/shard_map/ppermute | solution.py:351
  8.7 3.6 %collective-permute-start.2 = (bf16[896,256]{1,0:T(8,128)(2,1)}, bf16[896,256]{1,0:T(8,128)(2,1)S(1)}, u32[]{:S(2)}, u32[]{:S(2)}) collective-permute-start(bf16[896,256]{1,0:T(8,128)(2,1)} %pack.1), channel_id=1, source_target_pairs={{0,16},{1,65},{2,18},{3,67},{4,20},{5,69},{6,22},{7,71},{8,24},{9,... | collective-permute-start | bytes 1376264 | tf_op jit(solution)/shard_map/ppermute | solution.py:351
  12.3 1.0 collective-permute-start.3
  13.3 6.0 %collective-permute-done = bf16[896,256]{1,0:T(8,128)(2,1)S(1)} collective-permute-done((bf16[896,256]{1,0:T(8,128)(2,1)}, bf16[896,256]{1,0:T(8,128)(2,1)S(1)}, u32[]{:S(2)}, u32[]{:S(2)}) %collective-permute-start) | collective-permute-done | bytes 458784 | tf_op jit(solution)/shard_map/ppermute | solution.py:359
  19.2 4.6 %collective-permute-done.2 = bf16[896,256]{1,0:T(8,128)(2,1)S(1)} collective-permute-done((bf16[896,256]{1,0:T(8,128)(2,1)}, bf16[896,256]{1,0:T(8,128)(2,1)S(1)}, u32[]{:S(2)}, u32[]{:S(2)}) %collective-permute-start.2) | collective-permute-done | bytes 458784 | tf_op jit(solution)/shard_map/ppermute | solution.py:351
  23.8 1.2 pad_maximum_fusion.refs_8_.refs_9_
  25.1 1.6 %collective-permute-start.8 = (bf16[4,896,256]{2,1,0:T(8,128)(2,1)S(1)}, bf16[4,896,256]{2,1,0:T(8,128)(2,1)S(1)}, u32[]{:S(2)}, u32[]{:S(2)}) collective-permute-start(bf16[4,896,256]{2,1,0:T(8,128)(2,1)S(1)} %pad_maximum_fusion.refs_8_.refs_9_), channel_id=1, source_target_pairs={{0,32},{1,9},{2,34},{3,11},{4,36},{5,13},{6,38},{7,15},{8,40},{9,1... | collective-permute-start | bytes 5505032 | tf_op jit(solution)/shard_map/ppermute | solution.py:351
  26.7 1.7 %collective-permute-start.9 = (bf16[4,896,256]{2,1,0:T(8,128)(2,1)S(1)}, bf16[4,896,256]{2,1,0:T(8,128)(2,1)S(1)}, u32[]{:S(2)}, u32[]{:S(2)}) collective-permute-start(bf16[4,896,256]{2,1,0:T(8,128)(2,1)S(1)} %pad_maximum_fusion.refs_8_.refs_9_), channel_id=1, source_target_pairs={{0,96},{1,25},{2,98},{3,27},{4,100},{5,29},{6,102},{7,31},{8,104},... | collective-permute-start | bytes 5505032 | tf_op jit(solution)/shard_map/ppermute | solution.py:351
  28.4 1.4 collective-permute-start.5
  29.8 2.1 %collective-permute-start.6 = (bf16[896,256]{1,0:T(8,128)(2,1)S(1)}, bf16[896,256]{1,0:T(8,128)(2,1)S(1)}, u32[]{:S(2)}, u32[]{:S(2)}) collective-permute-start(bf16[896,256]{1,0:T(8,128)(2,1)S(1)} %collective-permute-done), channel_id=1, source_target_pairs={{0,16},{1,65},{2,18},{3,67},{4,20},{5,69},{6,22},{7,71},{8,24},{9,... | collective-permute-start | bytes 1376264 | tf_op jit(solution)/shard_map/ppermute | solution.py:351
  31.9 1.6 %collective-permute-start.7 = (bf16[896,256]{1,0:T(8,128)(2,1)S(1)}, bf16[896,256]{1,0:T(8,128)(2,1)S(1)}, u32[]{:S(2)}, u32[]{:S(2)}) collective-permute-start(bf16[896,256]{1,0:T(8,128)(2,1)S(1)} %collective-permute-done), channel_id=1, source_target_pairs={{0,24},{1,97},{2,26},{3,99},{4,28},{5,101},{6,30},{7,103},{8,0},{9... | collective-permute-start | bytes 1376264 | tf_op jit(solution)/shard_map/ppermute | solution.py:351
  33.5 9.5 %collective-permute-done.5 = bf16[896,256]{1,0:T(8,128)(2,1)S(1)} collective-permute-done((bf16[896,256]{1,0:T(8,128)(2,1)S(1)}, bf16[896,256]{1,0:T(8,128)(2,1)S(1)}, u32[]{:S(2)}, u32[]{:S(2)}) %collective-permute-start.5) | collective-permute-done | bytes 458784 | tf_op jit(solution)/shard_map/ppermute | solution.py:351
  43.1 10.1 %collective-permute-done.6 = bf16[896,256]{1,0:T(8,128)(2,1)S(1)} collective-permute-done((bf16[896,256]{1,0:T(8,128)(2,1)S(1)}, bf16[896,256]{1,0:T(8,128)(2,1)S(1)}, u32[]{:S(2)}, u32[]{:S(2)}) %collective-permute-start.6) | collective-permute-done | bytes 458784 | tf_op jit(solution)/shard_map/ppermute | solution.py:351
  53.2 0.6 collective-permute-done.7
  53.8 5.7 %collective-permute-done.8.refs_8_.refs_9_ = bf16[4,896,256]{2,1,0:T(8,128)(2,1)S(1)} collective-permute-done((bf16[4,896,256]{2,1,0:T(8,128)(2,1)S(1)}, bf16[4,896,256]{2,1,0:T(8,128)(2,1)S(1)}, u32[]{:S(2)}, u32[]{:S(2)}) %collective-permute-start.8) | collective-permute-done | bytes 1835040 | tf_op jit(solution)/shard_map/ppermute | solution.py:351
  59.4 0.4 collective-permute-done.9.refs_10_.refs_11_
  59.8 0.2 pad_maximum_fusion.1.refs_8_.refs_9_
  60.0 1.6 %collective-permute-start.11 = (bf16[4,896,256]{2,1,0:T(8,128)(2,1)S(1)}, bf16[4,896,256]{2,1,0:T(8,128)(2,1)S(1)}, u32[]{:S(2)}, u32[]{:S(2)}) collective-permute-start(bf16[4,896,256]{2,1,0:T(8,128)(2,1)S(1)} %pad_maximum_fusion.1.refs_8_.refs_9_), channel_id=1, source_target_pairs={{0,32},{1,9},{2,34},{3,11},{4,36},{5,13},{6,38},{7,15},{8,40},{9,1... | collective-permute-start | bytes 5505032 | tf_op jit(solution)/shard_map/ppermute | solution.py:351
  61.7 1.7 %collective-permute-start.12 = (bf16[4,896,256]{2,1,0:T(8,128)(2,1)S(1)}, bf16[4,896,256]{2,1,0:T(8,128)(2,1)}, u32[]{:S(2)}, u32[]{:S(2)}) collective-permute-start(bf16[4,896,256]{2,1,0:T(8,128)(2,1)S(1)} %pad_maximum_fusion.1.refs_8_.refs_9_), channel_id=1, source_target_pairs={{0,96},{1,25},{2,98},{3,27},{4,100},{5,29},{6,102},{7,31},{8,104},... | collective-permute-start | bytes 5505032 | tf_op jit(solution)/shard_map/ppermute | solution.py:351
  63.4 0.4 collective-permute-start.15
  63.9 2.9 %collective-permute-start.16 = (bf16[2,896,256]{2,1,0:T(8,128)(2,1)S(1)}, bf16[2,896,256]{2,1,0:T(8,128)(2,1)S(1)}, u32[]{:S(2)}, u32[]{:S(2)}) collective-permute-start(bf16[2,896,256]{2,1,0:T(8,128)(2,1)S(1)} %slice.18), channel_id=1, source_target_pairs={{0,96},{1,25},{2,98},{3,27},{4,100},{5,29},{6,102},{7,31},{8,104},... | collective-permute-start | bytes 2752520 | tf_op jit(solution)/shard_map/ppermute | solution.py:351
  66.8 6.4 %collective-permute-done.10.refs_6_.refs_7_ = bf16[256,16384]{1,0:T(8,128)(2,1)} collective-permute-done((bf16[256,16384]{1,0:T(8,128)(2,1)}, bf16[256,16384]{1,0:T(8,128)(2,1)}, u32[]{:S(2)}, u32[]{:S(2)}) %collective-permute-start.10) | collective-permute-done | bytes 8388640 | tf_op jit(solution)/shard_map/ppermute | solution.py:354
  73.3 4.5 %arrive.6 = (f32[512,768]{1,0:T(8,128)S(1)}, f32[256,32]{1,0:T(8,128)S(1)}, bf16[16,256,256]{2,1,0:T(8,128)(2,1)}) custom-call(s32[5]{0:T(128)S(1)} %copy-done.2, bf16[256,16384]{1,0:T(8,128)(2,1)} %tok.1, bf16[256,16384]{1,0:T(8,128)(2,1)} %tok.1, bf16[256,16384]{1,0:T(8,128)(2,1)} %refs_3_.11, bf16[256,16384]{1,0:T(8,128)(2,1)} %refs_3_.11, ...), custom_call_target="tpu_custom_call" | custom-call | flops 1073741824 | bytes 4194304 | tf_op jit(solution)/shard_map/arrive/pallas_call | solution.py:134
  77.8 6.7 %arrive.7 = (f32[512,768]{1,0:T(8,128)S(1)}, f32[256,32]{1,0:T(8,128)S(1)}, bf16[16,256,256]{2,1,0:T(8,128)(2,1)}) custom-call(s32[5]{0:T(128)S(1)} %copy-done.2, bf16[256,16384]{1,0:T(8,128)(2,1)} %tok.1, bf16[256,16384]{1,0:T(8,128)(2,1)} %tok.1, bf16[256,16384]{1,0:T(8,128)(2,1)} %refs_3_.11, ...), custom_call_target="tpu_custom_call", output_to_operand_aliasing={{0}: (13, {}), {1}: (14, {}), {2}: (15, {})} | custom-call | flops 2147483648 | bytes 8388608 | tf_op jit(solution)/shard_map/arrive/pallas_call | solution.py:134
  84.5 4.4 %arrive.8 = (f32[512,768]{1,0:T(8,128)S(1)}, f32[256,32]{1,0:T(8,128)S(1)}, bf16[16,256,256]{2,1,0:T(8,128)(2,1)}) custom-call(s32[5]{0:T(128)S(1)} %copy-done.2, bf16[256,16384]{1,0:T(8,128)(2,1)} %tok.1, bf16[256,16384]{1,0:T(8,128)(2,1)} %tok.1, bf16[256,16384]{1,0:T(8,128)(2,1)} %refs_3_.11, ...), custom_call_target="tpu_custom_call", output_to_operand_aliasing={{0}: (11, {}), {1}: (12, {})} | custom-call | flops 1073741824 | bytes 4194304 | tf_op jit(solution)/shard_map/arrive/pallas_call | solution.py:134
  88.9 1.8 %collective-permute-start.13 = (bf16[2,896,256]{2,1,0:T(8,128)(2,1)S(1)}, bf16[2,896,256]{2,1,0:T(8,128)(2,1)S(1)}, u32[]{:S(2)}, u32[]{:S(2)}) collective-permute-start(bf16[2,896,256]{2,1,0:T(8,128)(2,1)S(1)} %slice.15), channel_id=1, source_target_pairs={{0,32},{1,9},{2,34},{3,11},{4,36},{5,13},{6,38},{7,15},{8,40},{9,1... | collective-permute-start | bytes 2752520 | tf_op jit(solution)/shard_map/ppermute | solution.py:351
  90.7 1.2 slice.16
  92.0 1.7 %collective-permute-start.14 = (bf16[2,896,256]{2,1,0:T(8,128)(2,1)S(1)}, bf16[2,896,256]{2,1,0:T(8,128)(2,1)S(1)}, u32[]{:S(2)}, u32[]{:S(2)}) collective-permute-start(bf16[2,896,256]{2,1,0:T(8,128)(2,1)S(1)} %slice.16), channel_id=1, source_target_pairs={{0,96},{1,25},{2,98},{3,27},{4,100},{5,29},{6,102},{7,31},{8,104},... | collective-permute-start | bytes 2752520 | tf_op jit(solution)/shard_map/ppermute | solution.py:351
  93.7 7.3 %arrive.9 = (f32[512,768]{1,0:T(8,128)S(1)}, f32[256,32]{1,0:T(8,128)S(1)}, bf16[16,256,256]{2,1,0:T(8,128)(2,1)}) custom-call(s32[5]{0:T(128)S(1)} %copy-done.2, bf16[256,16384]{1,0:T(8,128)(2,1)} %tok.1, bf16[256,16384]{1,0:T(8,128)(2,1)} %tok.1, bf16[256,16384]{1,0:T(8,128)(2,1)} %refs_3_.11, ...), custom_call_target="tpu_custom_call", output_to_operand_aliasing={{0}: (13, {}), {1}: (14, {}), {2}: (15, {})} | custom-call | flops 2147483648 | bytes 8388608 | tf_op jit(solution)/shard_map/arrive/pallas_call | solution.py:134
  101.1 0.9 copy-done
  102.0 1.2 copy-done.1
  103.1 4.4 %arrive.10 = (f32[512,768]{1,0:T(8,128)S(1)}, f32[256,32]{1,0:T(8,128)S(1)}, bf16[16,256,256]{2,1,0:T(8,128)(2,1)}) custom-call(s32[5]{0:T(128)S(1)} %copy-done.2, bf16[256,16384]{1,0:T(8,128)(2,1)} %tok.1, bf16[256,16384]{1,0:T(8,128)(2,1)} %tok.1, bf16[256,16384]{1,0:T(8,128)(2,1)} %refs_3_.11, ...), custom_call_target="tpu_custom_call", output_to_operand_aliasing={{0}: (11, {}), {1}: (12, {}), {2}: (13, {})} | custom-call | flops 1073741824 | bytes 4194304 | tf_op jit(solution)/shard_map/arrive/pallas_call | solution.py:134
  107.5 4.4 %arrive.11 = (f32[512,768]{1,0:T(8,128)S(1)}, f32[256,32]{1,0:T(8,128)S(1)}, bf16[16,256,256]{2,1,0:T(8,128)(2,1)}) custom-call(s32[5]{0:T(128)S(1)} %copy-done.2, bf16[256,16384]{1,0:T(8,128)(2,1)} %tok.1, bf16[256,16384]{1,0:T(8,128)(2,1)} %tok.1, bf16[256,16384]{1,0:T(8,128)(2,1)} %refs_3_.11, ...), custom_call_target="tpu_custom_call", output_to_operand_aliasing={{0}: (11, {}), {1}: (12, {}), {2}: (13, {})} | custom-call | flops 1073741824 | bytes 4194304 | tf_op jit(solution)/shard_map/arrive/pallas_call | solution.py:134
  112.0 0.1 collective-permute-start.17
  112.1 2.3 %collective-permute-done.17.refs_2_ = f32[256,768]{1,0:T(8,128)S(1)} collective-permute-done((f32[256,768]{1,0:T(8,128)S(1)}, f32[256,768]{1,0:T(8,128)S(1)}, u32[]{:S(2)}, u32[]{:S(2)}) %collective-permute-start.17) | collective-permute-done | bytes 786464 | tf_op jit(solution)/shard_map/ppermute | solution.py:354
  114.4 0.1 collective-permute-start.18
  114.5 0.4 collective-permute-start.19
  115.5 0.1 pad_add_fusion.refs_0_
  115.6 1.7 %attend.1 = (bf16[256,256]{1,0:T(8,128)(2,1)S(1)}, bf16[32,256]{1,0:T(8,128)(2,1)S(1)}, bf16[16,512]{1,0:T(8,128)(2,1)S(1)}) custom-call(s32[2]{0:T(128)S(1)} %pad_add_fusion.refs_0_, f32[512,768]{1,0:T(8,128)S(1)} %get-tuple-element.75.refs_1_, f32[256,768]{1,0:T(8,128)S(1)} %collective-permute-done.17.refs_2_, f32[256,32]{1,0:T(8,128)S(1)} %get-tuple-element.79.refs_3_, ...), custom_call_target="tpu_custom_call" | custom-call | tf_op jit(solution)/shard_map/attend/pallas_call | solution.py:203
  117.4 5.9 %term.1 = bf16[32,48,512]{2,1,0:T(8,128)(2,1)} custom-call(bf16[32,256]{1,0:T(8,128)(2,1)S(1)} %get-tuple-element.80.mid, bf16[16,512]{1,0:T(8,128)(2,1)S(1)} %get-tuple-element.81.up_sum, bf16[256,16384]{1,0:T(8,128)(2,1)} %tok.1), custom_call_target="tpu_custom_call" | custom-call | tf_op jit(solution)/shard_map/term/pallas_call | solution.py:230
  123.3 6.1 %all-to-all-start = ((bf16[32,48,512]{2,1,0:T(8,128)(2,1)}), bf16[32,48,512]{2,1,0:T(8,128)(2,1)S(1)}, u32[]{:S(2)}, u32[]{:S(2)}) async-start(bf16[32,48,512]{2,1,0:T(8,128)(2,1)} %term.1), calls=%async_computation | async-start | bytes 3145728 | tf_op jit(solution)/shard_map/all_to_all | solution.py:412
  129.5 14.7 %output.1 = bf16[256,16384]{1,0:T(8,128)(2,1)} custom-call(s32[5]{0:T(128)S(1)} %copy-done.2, bf16[256,256]{1,0:T(8,128)(2,1)S(1)} %get-tuple-element.82.context, bf16[16,256,256]{2,1,0:T(8,128)(2,1)} %get-tuple-element.83.own, bf16[16,256,256]{2,1,0:T(8,128)(2,1)} %get-tuple-element.84.flipped, bf16[16,256,256]{2,1,0:T(8,128)(2,1)} %collective-permute-done.18.their_own, ...), custom_call_target="tpu_custom_call" | custom-call | flops 2147483648 | bytes 16777216 | tf_op jit(solution)/shard_map/output/pallas_call | solution.py:273
  144.2 11.6 %all-to-all-done.got = bf16[32,48,512]{2,1,0:T(8,128)(2,1)S(1)} async-done(((bf16[32,48,512]{2,1,0:T(8,128)(2,1)}), bf16[32,48,512]{2,1,0:T(8,128)(2,1)S(1)}, u32[]{:S(2)}, u32[]{:S(2)}) %all-to-all-start) | async-done | bytes 1572896 | tf_op jit(solution)/shard_map/all_to_all | solution.py:412
  155.8 1.2 total.1
  (25 shorter events, 0.3 us)
Async XLA Ops:
  0.6 23.2 %collective-permute-start.4 = (bf16[256,16384]{1,0:T(8,128)(2,1)}, bf16[256,16384]{1,0:T(8,128)(2,1)}, u32[]{:S(2)}, u32[]{:S(2)}) collective-permute-start(bf16[256,16384]{1,0:T(8,128)(2,1)} %tok.1), channel_id=1, source_target_pairs={{0,1},{1,0},{2,3},{3,2},{4,5},{5,4},{6,7},{7,6},{8,9},{9,8},{10,11... | collective-permute-start | bytes 25165832 | tf_op jit(solution)/shard_map/ppermute | solution.py:354
  4.6 14.6 %collective-permute-start = (bf16[896,256]{1,0:T(8,128)(2,1)}, bf16[896,256]{1,0:T(8,128)(2,1)S(1)}, u32[]{:S(2)}, u32[]{:S(2)}) collective-permute-start(bf16[896,256]{1,0:T(8,128)(2,1)} %pack.1), channel_id=1, source_target_pairs={{0,4},{4,0},{8,12},{12,8},{16,20},{20,16},{24,28},{28,24},{32,36},... | collective-permute-start | bytes 1376264 | tf_op jit(solution)/shard_map/ppermute | solution.py:359
  6.8 12.5 %collective-permute-start.1 = (bf16[896,256]{1,0:T(8,128)(2,1)}, bf16[896,256]{1,0:T(8,128)(2,1)S(1)}, u32[]{:S(2)}, u32[]{:S(2)}) collective-permute-start(bf16[896,256]{1,0:T(8,128)(2,1)} %pack.1), channel_id=1, source_target_pairs={{0,8},{1,33},{2,10},{3,35},{4,12},{5,37},{6,14},{7,39},{8,16},{9,4... | collective-permute-start | bytes 1376264 | tf_op jit(solution)/shard_map/ppermute | solution.py:351
  8.7 15.2 %collective-permute-start.2 = (bf16[896,256]{1,0:T(8,128)(2,1)}, bf16[896,256]{1,0:T(8,128)(2,1)S(1)}, u32[]{:S(2)}, u32[]{:S(2)}) collective-permute-start(bf16[896,256]{1,0:T(8,128)(2,1)} %pack.1), channel_id=1, source_target_pairs={{0,16},{1,65},{2,18},{3,67},{4,20},{5,69},{6,22},{7,71},{8,24},{9,... | collective-permute-start | bytes 1376264 | tf_op jit(solution)/shard_map/ppermute | solution.py:351
  12.3 11.6 %collective-permute-start.3 = (bf16[896,256]{1,0:T(8,128)(2,1)}, bf16[896,256]{1,0:T(8,128)(2,1)S(1)}, u32[]{:S(2)}, u32[]{:S(2)}) collective-permute-start(bf16[896,256]{1,0:T(8,128)(2,1)} %pack.1), channel_id=1, source_target_pairs={{0,24},{1,97},{2,26},{3,99},{4,28},{5,101},{6,30},{7,103},{8,0},{9... | collective-permute-start | bytes 1376264 | tf_op jit(solution)/shard_map/ppermute | solution.py:351
  25.1 34.3 %collective-permute-start.8 = (bf16[4,896,256]{2,1,0:T(8,128)(2,1)S(1)}, bf16[4,896,256]{2,1,0:T(8,128)(2,1)S(1)}, u32[]{:S(2)}, u32[]{:S(2)}) collective-permute-start(bf16[4,896,256]{2,1,0:T(8,128)(2,1)S(1)} %pad_maximum_fusion.refs_8_.refs_9_), channel_id=1, source_target_pairs={{0,32},{1,9},{2,34},{3,11},{4,36},{5,13},{6,38},{7,15},{8,40},{9,1... | collective-permute-start | bytes 5505032 | tf_op jit(solution)/shard_map/ppermute | solution.py:351
  26.7 33.1 %collective-permute-start.9 = (bf16[4,896,256]{2,1,0:T(8,128)(2,1)S(1)}, bf16[4,896,256]{2,1,0:T(8,128)(2,1)S(1)}, u32[]{:S(2)}, u32[]{:S(2)}) collective-permute-start(bf16[4,896,256]{2,1,0:T(8,128)(2,1)S(1)} %pad_maximum_fusion.refs_8_.refs_9_), channel_id=1, source_target_pairs={{0,96},{1,25},{2,98},{3,27},{4,100},{5,29},{6,102},{7,31},{8,104},... | collective-permute-start | bytes 5505032 | tf_op jit(solution)/shard_map/ppermute | solution.py:351
  28.4 14.7 %collective-permute-start.5 = (bf16[896,256]{1,0:T(8,128)(2,1)S(1)}, bf16[896,256]{1,0:T(8,128)(2,1)S(1)}, u32[]{:S(2)}, u32[]{:S(2)}) collective-permute-start(bf16[896,256]{1,0:T(8,128)(2,1)S(1)} %collective-permute-done), channel_id=1, source_target_pairs={{0,8},{1,33},{2,10},{3,35},{4,12},{5,37},{6,14},{7,39},{8,16},{9,4... | collective-permute-start | bytes 1376264 | tf_op jit(solution)/shard_map/ppermute | solution.py:351
  29.8 23.4 %collective-permute-start.6 = (bf16[896,256]{1,0:T(8,128)(2,1)S(1)}, bf16[896,256]{1,0:T(8,128)(2,1)S(1)}, u32[]{:S(2)}, u32[]{:S(2)}) collective-permute-start(bf16[896,256]{1,0:T(8,128)(2,1)S(1)} %collective-permute-done), channel_id=1, source_target_pairs={{0,16},{1,65},{2,18},{3,67},{4,20},{5,69},{6,22},{7,71},{8,24},{9,... | collective-permute-start | bytes 1376264 | tf_op jit(solution)/shard_map/ppermute | solution.py:351
  31.9 21.8 %collective-permute-start.7 = (bf16[896,256]{1,0:T(8,128)(2,1)S(1)}, bf16[896,256]{1,0:T(8,128)(2,1)S(1)}, u32[]{:S(2)}, u32[]{:S(2)}) collective-permute-start(bf16[896,256]{1,0:T(8,128)(2,1)S(1)} %collective-permute-done), channel_id=1, source_target_pairs={{0,24},{1,97},{2,26},{3,99},{4,28},{5,101},{6,30},{7,103},{8,0},{9... | collective-permute-start | bytes 1376264 | tf_op jit(solution)/shard_map/ppermute | solution.py:351
  59.8 13.5 %collective-permute-start.10 = (bf16[256,16384]{1,0:T(8,128)(2,1)}, bf16[256,16384]{1,0:T(8,128)(2,1)}, u32[]{:S(2)}, u32[]{:S(2)}) collective-permute-start(bf16[256,16384]{1,0:T(8,128)(2,1)} %refs_3_.11), channel_id=1, source_target_pairs={{0,1},{1,0},{2,3},{3,2},{4,5},{5,4},{6,7},{7,6},{8,9},{9,8},{10,11... | collective-permute-start | bytes 25165832 | tf_op jit(solution)/shard_map/ppermute | solution.py:354
  60.0 13.3 %copy-start.2 = (s32[5]{0:T(128)S(1)}, s32[5]{0:T(128)}, u32[]{:S(2)}) copy-start(s32[5]{0:T(128)} %stack.53.where) | copy-start | bytes 64
  60.0 28.8 %collective-permute-start.11 = (bf16[4,896,256]{2,1,0:T(8,128)(2,1)S(1)}, bf16[4,896,256]{2,1,0:T(8,128)(2,1)S(1)}, u32[]{:S(2)}, u32[]{:S(2)}) collective-permute-start(bf16[4,896,256]{2,1,0:T(8,128)(2,1)S(1)} %pad_maximum_fusion.1.refs_8_.refs_9_), channel_id=1, source_target_pairs={{0,32},{1,9},{2,34},{3,11},{4,36},{5,13},{6,38},{7,15},{8,40},{9,1... | collective-permute-start | bytes 5505032 | tf_op jit(solution)/shard_map/ppermute | solution.py:351
  61.7 27.1 %collective-permute-start.12 = (bf16[4,896,256]{2,1,0:T(8,128)(2,1)S(1)}, bf16[4,896,256]{2,1,0:T(8,128)(2,1)}, u32[]{:S(2)}, u32[]{:S(2)}) collective-permute-start(bf16[4,896,256]{2,1,0:T(8,128)(2,1)S(1)} %pad_maximum_fusion.1.refs_8_.refs_9_), channel_id=1, source_target_pairs={{0,96},{1,25},{2,98},{3,27},{4,100},{5,29},{6,102},{7,31},{8,104},... | collective-permute-start | bytes 5505032 | tf_op jit(solution)/shard_map/ppermute | solution.py:351
  63.4 37.6 %collective-permute-start.15 = (bf16[2,896,256]{2,1,0:T(8,128)(2,1)S(1)}, bf16[2,896,256]{2,1,0:T(8,128)(2,1)S(1)}, u32[]{:S(2)}, u32[]{:S(2)}) collective-permute-start(bf16[2,896,256]{2,1,0:T(8,128)(2,1)S(1)} %slice.17), channel_id=1, source_target_pairs={{0,32},{1,9},{2,34},{3,11},{4,36},{5,13},{6,38},{7,15},{8,40},{9,1... | collective-permute-start | bytes 2752520 | tf_op jit(solution)/shard_map/ppermute | solution.py:351
  63.9 37.1 %collective-permute-start.16 = (bf16[2,896,256]{2,1,0:T(8,128)(2,1)S(1)}, bf16[2,896,256]{2,1,0:T(8,128)(2,1)S(1)}, u32[]{:S(2)}, u32[]{:S(2)}) collective-permute-start(bf16[2,896,256]{2,1,0:T(8,128)(2,1)S(1)} %slice.18), channel_id=1, source_target_pairs={{0,96},{1,25},{2,98},{3,27},{4,100},{5,29},{6,102},{7,31},{8,104},... | collective-permute-start | bytes 2752520 | tf_op jit(solution)/shard_map/ppermute | solution.py:351
  88.9 18.6 %collective-permute-start.13 = (bf16[2,896,256]{2,1,0:T(8,128)(2,1)S(1)}, bf16[2,896,256]{2,1,0:T(8,128)(2,1)S(1)}, u32[]{:S(2)}, u32[]{:S(2)}) collective-permute-start(bf16[2,896,256]{2,1,0:T(8,128)(2,1)S(1)} %slice.15), channel_id=1, source_target_pairs={{0,32},{1,9},{2,34},{3,11},{4,36},{5,13},{6,38},{7,15},{8,40},{9,1... | collective-permute-start | bytes 2752520 | tf_op jit(solution)/shard_map/ppermute | solution.py:351
  92.0 15.5 %collective-permute-start.14 = (bf16[2,896,256]{2,1,0:T(8,128)(2,1)S(1)}, bf16[2,896,256]{2,1,0:T(8,128)(2,1)S(1)}, u32[]{:S(2)}, u32[]{:S(2)}) collective-permute-start(bf16[2,896,256]{2,1,0:T(8,128)(2,1)S(1)} %slice.16), channel_id=1, source_target_pairs={{0,96},{1,25},{2,98},{3,27},{4,100},{5,29},{6,102},{7,31},{8,104},... | collective-permute-start | bytes 2752520 | tf_op jit(solution)/shard_map/ppermute | solution.py:351
  101.0 0.9 copy-start
  102.0 1.2 copy-start.1
  107.5 8.1 %copy-start.3 = (bf16[2,16,384]{2,1,0:T(8,128)(2,1)S(1)}, bf16[2,16,384]{2,1,0:T(8,128)(2,1)}, u32[]{:S(2)}) copy-start(bf16[2,16,384]{2,1,0:T(8,128)(2,1)} %param.17) | copy-start | bytes 73732
  112.0 2.4 %collective-permute-start.17 = (f32[256,768]{1,0:T(8,128)S(1)}, f32[256,768]{1,0:T(8,128)S(1)}, u32[]{:S(2)}, u32[]{:S(2)}) collective-permute-start(f32[256,768]{1,0:T(8,128)S(1)} %slice.19), channel_id=1, source_target_pairs={{0,1},{1,0},{2,3},{3,2},{4,5},{5,4},{6,7},{7,6},{8,9},{9,8},{10,11... | collective-permute-start | bytes 2359304 | tf_op jit(solution)/shard_map/ppermute | solution.py:354
  114.4 15.1 %collective-permute-start.18 = (bf16[16,256,256]{2,1,0:T(8,128)(2,1)}, bf16[16,256,256]{2,1,0:T(8,128)(2,1)}, u32[]{:S(2)}, u32[]{:S(2)}) collective-permute-start(bf16[16,256,256]{2,1,0:T(8,128)(2,1)} %get-tuple-element.83.own), channel_id=1, source_target_pairs={{0,1},{1,0},{2,3},{3,2},{4,5},{5,4},{6,7},{7,6},{8,9},{9,8},{10,11... | collective-permute-start | bytes 6291464 | tf_op jit(solution)/shard_map/ppermute | solution.py:354
  114.5 15.0 %collective-permute-start.19 = (bf16[16,256,256]{2,1,0:T(8,128)(2,1)}, bf16[16,256,256]{2,1,0:T(8,128)(2,1)}, u32[]{:S(2)}, u32[]{:S(2)}) collective-permute-start(bf16[16,256,256]{2,1,0:T(8,128)(2,1)} %get-tuple-element.84.flipped), channel_id=1, source_target_pairs={{0,1},{1,0},{2,3},{3,2},{4,5},{5,4},{6,7},{7,6},{8,9},{9,8},{10,11... | collective-permute-start | bytes 6291464 | tf_op jit(solution)/shard_map/ppermute | solution.py:354
  123.3 32.6 %all-to-all-start = ((bf16[32,48,512]{2,1,0:T(8,128)(2,1)}), bf16[32,48,512]{2,1,0:T(8,128)(2,1)S(1)}, u32[]{:S(2)}, u32[]{:S(2)}) async-start(bf16[32,48,512]{2,1,0:T(8,128)(2,1)} %term.1), calls=%async_computation | async-start | bytes 3145728 | tf_op jit(solution)/shard_map/all_to_all | solution.py:412

commit v4 on v3

--- a/solution.py
+++ b/solution.py
@@ -118,7 +118,9 @@
     rows, half = pieces[0][0].shape[1:]
 
     def at(k, w, p):
-        late = jnp.where(k < 2, lates[0], lates[-1])
+        late = jnp.int32(lates[0])
+        for i in range(1, len(lates)):
+            late = jnp.where(k >= 2 * i, lates[i], late)
         return 2 * place(w, 2 * (k % 2) + p, late) + (w[2] ^ flip)
 
     def two(cols, index):
@@ -387,9 +389,9 @@
     def halves(array):
         return [(array, 0), (array, 1)]
 
-    *sums, kept = add(halves(own), (0,), 0, 0, (None, None, None))
     own_far = shift(own_ahead[:2], 1, True), shift(own_behind[2:], -1, True)
-    *sums, kept = add(halves(own_ahead) + halves(own_behind), (1, 3), 0, 2, (*sums, kept))
+    here = halves(own) + halves(own_ahead) + halves(own_behind)
+    *sums, kept = add(here, (0, 1, 3), 0, 0, (None, None, None))
     *sums, kept_flip = add(halves(flip), (0,), 1, 0, (*sums, None))
     flip_ahead, flip_behind, sums = lax.optimization_barrier((flip_ahead, flip_behind, sums))
     flip_far = shift(flip_ahead[:2], 1, True), shift(flip_behind[2:], -1, True)

time: 158 us -> 158 us (level)
  waiting for transfers between devices: 57.2 us -> 67.1 us
  starting transfers between devices: 34.2 us -> 29.1 us
  local copies, waits for them, and re-layouts: 4.24 us -> 0.99 us
  Pallas kernels: 57.7 us -> 55.7 us
    ppermute x14, waiting for transfers between devices: 30.9 us -> 44.7 us  [shift(): return lax.ppermute(array, ('fsdp', 'tenant'), to)]
    ppermute x1, waiting for transfers between devices: 5.97 us -> 0.01 us  [body(): flipped = lax.ppermute(piece, 'fsdp', [(f, f ^ 1) for f in range(parts)])]
    ppermute x14, starting transfers between devices: 25.2 us -> 19.9 us  [shift(): return lax.ppermute(array, ('fsdp', 'tenant'), to)]
    ppermute x5, waiting for transfers between devices: 8.73 us -> 10.8 us  [swap(): return lax.ppermute(array, 'tenant', [(t, t ^ 1) for t in range(tenants)])]
    unnamed x8 -> x6, local copies, waits for them, and re-layouts: 2.11 us -> 0.01 us
    pallas_call x6 -> x5, Pallas kernels: 31.6 us -> 29.6 us  [arrive(): pl.pallas_call(functools.partial(arrive_kernel, pieces=len(pieces), fresh...]
  transfers between devices with their start and end apart: 21 -> 21, of which waited for: 10 -> 11; matrix products, arithmetic and copies ran while one was open for 2% -> 1% of each run, Pallas kernels for 33% -> 32%
where the time goes in v4:
time: 158 us; the launch traced here: 157 us
  waiting for transfers between devices  67.1 us (42%)
  Pallas kernels  55.7 us (35%)
  starting transfers between devices  29.1 us (18%)
  between operations  2.14 us (1%)
  other arithmetic  1.58 us (1%)
    ppermute x14, waiting for transfers between devices, shift(): return lax.ppermute(array, ('fsdp', 'tenant'), to)  44.7 us
    pallas_call x5, Pallas kernels, arrive(): pl.pallas_call(functools.partial(arrive_kernel, pieces=len(pieces), fresh...  29.6 us
    ppermute x14, starting transfers between devices, shift(): return lax.ppermute(array, ('fsdp', 'tenant'), to)  19.9 us
    pallas_call x1, Pallas kernels, output_of(): pl.pallas_call(output_kernel, grid_spec=pltpu.PrefetchScalarGridSpec(num_...  14.8 us
    all_to_all x1, waiting for transfers between devices, body(): got = lax.all_to_all(sent, 'fsdp', split_axis=0, concat_axis=0, tiled=True)  11.7 us
    ppermute x5, waiting for transfers between devices, swap(): return lax.ppermute(array, 'tenant', [(t, t ^ 1) for t in range(tenants)])  10.8 us
    pallas_call x1, Pallas kernels, term(): pl.pallas_call(term_kernel, grid=(parts // per,), in_specs=[pl.BlockSpec(...  5.93 us
    all_to_all x1, starting transfers between devices, body(): got = lax.all_to_all(sent, 'fsdp', split_axis=0, concat_axis=0, tiled=True)  5.25 us
  transfers between devices with their start and end apart: 21, of which 11 were waited for; matrix products, arithmetic and copies ran while one was open for 1% of the time, Pallas kernels for 32%

profile of v4, /device:TPU:2, one launch (start us, length us, event | category | flops | bytes accessed | tf_op | source)
XLA Modules:
  0.0 156.7 jit_solution(17928475048964229271)
XLA Ops:
  0.6 0.1 collective-permute-start.4
  1.4 0.7 stack.53.where
  2.1 2.5 %pack.1 = bf16[896,256]{1,0:T(8,128)(2,1)} custom-call(s32[5]{0:T(128)} %stack.53.where, bf16[512,256]{1,0:T(8,128)(2,1)} %w_query.1, bf16[512,128]{1,0:T(8,128)(2,1)} %w_key.1, bf16[512,128]{1,0:T(8,128)(2,1)} %w_value.1, bf16[64,512]{1,0:T(8,128)(2,1)} %bitcast.35, bf16[256,512]{1,0:T(8,128)(2,1)} %w_output.1), custom_call_target="tpu_custom_call" | custom-call | tf_op jit(solution)/shard_map/pack/pallas_call | solution.py:42
  4.6 4.0 %collective-permute-start.3 = (bf16[896,256]{1,0:T(8,128)(2,1)}, bf16[896,256]{1,0:T(8,128)(2,1)S(1)}, u32[]{:S(2)}, u32[]{:S(2)}) collective-permute-start(bf16[896,256]{1,0:T(8,128)(2,1)} %pack.1), channel_id=1, source_target_pairs={{0,24},{1,97},{2,26},{3,99},{4,28},{5,101},{6,30},{7,103},{8,0},{9... | collective-permute-start | bytes 1376264 | tf_op jit(solution)/shard_map/ppermute | solution.py:353
  8.7 1.3 collective-permute-start.1
  9.9 2.1 %collective-permute-start = (bf16[896,256]{1,0:T(8,128)(2,1)}, bf16[896,256]{1,0:T(8,128)(2,1)S(1)}, u32[]{:S(2)}, u32[]{:S(2)}) collective-permute-start(bf16[896,256]{1,0:T(8,128)(2,1)} %pack.1), channel_id=1, source_target_pairs={{0,4},{4,0},{8,12},{12,8},{16,20},{20,16},{24,28},{28,24},{32,36},... | collective-permute-start | bytes 1376264 | tf_op jit(solution)/shard_map/ppermute | solution.py:361
  12.1 7.8 %collective-permute-done.3 = bf16[896,256]{1,0:T(8,128)(2,1)S(1)} collective-permute-done((bf16[896,256]{1,0:T(8,128)(2,1)}, bf16[896,256]{1,0:T(8,128)(2,1)S(1)}, u32[]{:S(2)}, u32[]{:S(2)}) %collective-permute-start.3) | collective-permute-done | bytes 458784 | tf_op jit(solution)/shard_map/ppermute | solution.py:353
  19.9 0.0 collective-permute-done.2
  19.9 3.6 %collective-permute-done.1 = bf16[896,256]{1,0:T(8,128)(2,1)S(1)} collective-permute-done((bf16[896,256]{1,0:T(8,128)(2,1)}, bf16[896,256]{1,0:T(8,128)(2,1)S(1)}, u32[]{:S(2)}, u32[]{:S(2)}) %collective-permute-start.1) | collective-permute-done | bytes 458784 | tf_op jit(solution)/shard_map/ppermute | solution.py:353
  23.5 1.2 pad_maximum_fusion.refs_8_.refs_9_
  24.8 3.1 %collective-permute-start.9 = (bf16[4,896,256]{2,1,0:T(8,128)(2,1)S(1)}, bf16[4,896,256]{2,1,0:T(8,128)(2,1)S(1)}, u32[]{:S(2)}, u32[]{:S(2)}) collective-permute-start(bf16[4,896,256]{2,1,0:T(8,128)(2,1)S(1)} %pad_maximum_fusion.refs_8_.refs_9_), channel_id=1, source_target_pairs={{0,96},{1,25},{2,98},{3,27},{4,100},{5,29},{6,102},{7,31},{8,104},... | collective-permute-start | bytes 5505032 | tf_op jit(solution)/shard_map/ppermute | solution.py:353
  27.9 2.8 %collective-permute-start.7 = (bf16[896,256]{1,0:T(8,128)(2,1)S(1)}, bf16[896,256]{1,0:T(8,128)(2,1)S(1)}, u32[]{:S(2)}, u32[]{:S(2)}) collective-permute-start(bf16[896,256]{1,0:T(8,128)(2,1)S(1)} %collective-permute-done), channel_id=1, source_target_pairs={{0,24},{1,97},{2,26},{3,99},{4,28},{5,101},{6,30},{7,103},{8,0},{9... | collective-permute-start | bytes 1376264 | tf_op jit(solution)/shard_map/ppermute | solution.py:353
  30.7 1.3 collective-permute-start.5
  31.9 10.6 %collective-permute-done.7 = bf16[896,256]{1,0:T(8,128)(2,1)S(1)} collective-permute-done((bf16[896,256]{1,0:T(8,128)(2,1)S(1)}, bf16[896,256]{1,0:T(8,128)(2,1)S(1)}, u32[]{:S(2)}, u32[]{:S(2)}) %collective-permute-start.7) | collective-permute-done | bytes 458784 | tf_op jit(solution)/shard_map/ppermute | solution.py:353
  42.5 3.1 %collective-permute-done.6 = bf16[896,256]{1,0:T(8,128)(2,1)S(1)} collective-permute-done((bf16[896,256]{1,0:T(8,128)(2,1)S(1)}, bf16[896,256]{1,0:T(8,128)(2,1)S(1)}, u32[]{:S(2)}, u32[]{:S(2)}) %collective-permute-start.6) | collective-permute-done | bytes 458784 | tf_op jit(solution)/shard_map/ppermute | solution.py:353
  45.6 5.8 %collective-permute-done.5 = bf16[896,256]{1,0:T(8,128)(2,1)S(1)} collective-permute-done((bf16[896,256]{1,0:T(8,128)(2,1)S(1)}, bf16[896,256]{1,0:T(8,128)(2,1)S(1)}, u32[]{:S(2)}, u32[]{:S(2)}) %collective-permute-start.5) | collective-permute-done | bytes 458784 | tf_op jit(solution)/shard_map/ppermute | solution.py:353
  51.5 7.0 %collective-permute-done.9.refs_12_.refs_13_ = bf16[4,896,256]{2,1,0:T(8,128)(2,1)S(1)} collective-permute-done((bf16[4,896,256]{2,1,0:T(8,128)(2,1)S(1)}, bf16[4,896,256]{2,1,0:T(8,128)(2,1)S(1)}, u32[]{:S(2)}, u32[]{:S(2)}) %collective-permute-start.9) | collective-permute-done | bytes 1835040 | tf_op jit(solution)/shard_map/ppermute | solution.py:353
  58.4 3.7 %collective-permute-done.8.refs_10_.refs_11_ = bf16[4,896,256]{2,1,0:T(8,128)(2,1)S(1)} collective-permute-done((bf16[4,896,256]{2,1,0:T(8,128)(2,1)S(1)}, bf16[4,896,256]{2,1,0:T(8,128)(2,1)S(1)}, u32[]{:S(2)}, u32[]{:S(2)}) %collective-permute-start.8) | collective-permute-done | bytes 1835040 | tf_op jit(solution)/shard_map/ppermute | solution.py:353
  62.1 0.2 pad_maximum_fusion.1.refs_8_.refs_9_
  62.4 0.9 collective-permute-start.12
  63.2 1.2 collective-permute-start.11
  64.5 0.1 slice.17
  64.5 0.1 slice.18
  64.6 2.1 %collective-permute-start.16 = (bf16[2,896,256]{2,1,0:T(8,128)(2,1)S(1)}, bf16[2,896,256]{2,1,0:T(8,128)(2,1)S(1)}, u32[]{:S(2)}, u32[]{:S(2)}) collective-permute-start(bf16[2,896,256]{2,1,0:T(8,128)(2,1)S(1)} %slice.18), channel_id=1, source_target_pairs={{0,96},{1,25},{2,98},{3,27},{4,100},{5,29},{6,102},{7,31},{8,104},... | collective-permute-start | bytes 2752520 | tf_op jit(solution)/shard_map/ppermute | solution.py:353
  66.7 0.0 collective-permute-start.15
  66.7 8.9 %collective-permute-done.10.refs_6_.refs_7_ = bf16[256,16384]{1,0:T(8,128)(2,1)} collective-permute-done((bf16[256,16384]{1,0:T(8,128)(2,1)}, bf16[256,16384]{1,0:T(8,128)(2,1)}, u32[]{:S(2)}, u32[]{:S(2)}) %collective-permute-start.10) | collective-permute-done | bytes 8388640 | tf_op jit(solution)/shard_map/ppermute | solution.py:356
  75.6 9.7 %arrive.5 = (f32[512,768]{1,0:T(8,128)S(1)}, f32[256,32]{1,0:T(8,128)S(1)}, bf16[16,256,256]{2,1,0:T(8,128)(2,1)}) custom-call(s32[5]{0:T(128)S(1)} %copy-done, bf16[256,16384]{1,0:T(8,128)(2,1)} %tok.1, bf16[256,16384]{1,0:T(8,128)(2,1)} %tok.1, bf16[256,16384]{1,0:T(8,128)(2,1)} %refs_3_.9, bf16[256,16384]{1,0:T(8,128)(2,1)} %refs_3_.9, ...), custom_call_target="tpu_custom_call" | custom-call | flops 3221225472 | bytes 12582912 | tf_op jit(solution)/shard_map/arrive/pallas_call | solution.py:136
  85.4 4.4 %arrive.6 = (f32[512,768]{1,0:T(8,128)S(1)}, f32[256,32]{1,0:T(8,128)S(1)}, bf16[16,256,256]{2,1,0:T(8,128)(2,1)}) custom-call(s32[5]{0:T(128)S(1)} %copy-done, bf16[256,16384]{1,0:T(8,128)(2,1)} %tok.1, bf16[256,16384]{1,0:T(8,128)(2,1)} %tok.1, bf16[256,16384]{1,0:T(8,128)(2,1)} %refs_3_.9, ...), custom_call_target="tpu_custom_call", output_to_operand_aliasing={{0}: (11, {}), {1}: (12, {})} | custom-call | flops 1073741824 | bytes 4194304 | tf_op jit(solution)/shard_map/arrive/pallas_call | solution.py:136
  89.8 0.1 slice.16
  89.8 0.1 slice.15
  89.9 0.2 collective-permute-start.13
  90.1 3.1 %collective-permute-start.14 = (bf16[2,896,256]{2,1,0:T(8,128)(2,1)S(1)}, bf16[2,896,256]{2,1,0:T(8,128)(2,1)S(1)}, u32[]{:S(2)}, u32[]{:S(2)}) collective-permute-start(bf16[2,896,256]{2,1,0:T(8,128)(2,1)S(1)} %slice.16), channel_id=1, source_target_pairs={{0,96},{1,25},{2,98},{3,27},{4,100},{5,29},{6,102},{7,31},{8,104},... | collective-permute-start | bytes 2752520 | tf_op jit(solution)/shard_map/ppermute | solution.py:353
  93.2 6.7 %arrive.7 = (f32[512,768]{1,0:T(8,128)S(1)}, f32[256,32]{1,0:T(8,128)S(1)}, bf16[16,256,256]{2,1,0:T(8,128)(2,1)}) custom-call(s32[5]{0:T(128)S(1)} %copy-done, bf16[256,16384]{1,0:T(8,128)(2,1)} %tok.1, bf16[256,16384]{1,0:T(8,128)(2,1)} %tok.1, bf16[256,16384]{1,0:T(8,128)(2,1)} %refs_3_.9, ...), custom_call_target="tpu_custom_call", output_to_operand_aliasing={{0}: (13, {}), {1}: (14, {}), {2}: (15, {})} | custom-call | flops 2147483648 | bytes 8388608 | tf_op jit(solution)/shard_map/arrive/pallas_call | solution.py:136
  99.9 4.4 %arrive.8 = (f32[512,768]{1,0:T(8,128)S(1)}, f32[256,32]{1,0:T(8,128)S(1)}, bf16[16,256,256]{2,1,0:T(8,128)(2,1)}) custom-call(s32[5]{0:T(128)S(1)} %copy-done, bf16[256,16384]{1,0:T(8,128)(2,1)} %tok.1, bf16[256,16384]{1,0:T(8,128)(2,1)} %tok.1, bf16[256,16384]{1,0:T(8,128)(2,1)} %refs_3_.9, ...), custom_call_target="tpu_custom_call", output_to_operand_aliasing={{0}: (11, {}), {1}: (12, {}), {2}: (13, {})} | custom-call | flops 1073741824 | bytes 4194304 | tf_op jit(solution)/shard_map/arrive/pallas_call | solution.py:136
  104.3 3.0 %collective-permute-done.13.refs_8_ = bf16[2,896,256]{2,1,0:T(8,128)(2,1)S(1)} collective-permute-done((bf16[2,896,256]{2,1,0:T(8,128)(2,1)S(1)}, bf16[2,896,256]{2,1,0:T(8,128)(2,1)S(1)}, u32[]{:S(2)}, u32[]{:S(2)}) %collective-permute-start.13) | collective-permute-done | bytes 917536 | tf_op jit(solution)/shard_map/ppermute | solution.py:353
  107.3 4.4 %arrive.9 = (f32[512,768]{1,0:T(8,128)S(1)}, f32[256,32]{1,0:T(8,128)S(1)}, bf16[16,256,256]{2,1,0:T(8,128)(2,1)}) custom-call(s32[5]{0:T(128)S(1)} %copy-done, bf16[256,16384]{1,0:T(8,128)(2,1)} %tok.1, bf16[256,16384]{1,0:T(8,128)(2,1)} %tok.1, bf16[256,16384]{1,0:T(8,128)(2,1)} %refs_3_.9, ...), custom_call_target="tpu_custom_call", output_to_operand_aliasing={{0}: (11, {}), {1}: (12, {}), {2}: (13, {})} | custom-call | flops 1073741824 | bytes 4194304 | tf_op jit(solution)/shard_map/arrive/pallas_call | solution.py:136
  111.7 0.1 slice.19
  111.8 1.2 collective-permute-start.17
  112.9 1.9 %collective-permute-done.17.refs_2_ = f32[256,768]{1,0:T(8,128)S(1)} collective-permute-done((f32[256,768]{1,0:T(8,128)S(1)}, f32[256,768]{1,0:T(8,128)S(1)}, u32[]{:S(2)}, u32[]{:S(2)}) %collective-permute-start.17) | collective-permute-done | bytes 786464 | tf_op jit(solution)/shard_map/ppermute | solution.py:356
  114.8 0.4 collective-permute-start.18
  115.2 0.1 collective-permute-start.19
  116.0 0.1 pad_add_fusion.refs_0_
  116.1 1.7 %attend.1 = (bf16[256,256]{1,0:T(8,128)(2,1)S(1)}, bf16[32,256]{1,0:T(8,128)(2,1)S(1)}, bf16[16,512]{1,0:T(8,128)(2,1)S(1)}) custom-call(s32[2]{0:T(128)S(1)} %pad_add_fusion.refs_0_, f32[512,768]{1,0:T(8,128)S(1)} %get-tuple-element.69.refs_1_, f32[256,768]{1,0:T(8,128)S(1)} %collective-permute-done.17.refs_2_, f32[256,32]{1,0:T(8,128)S(1)} %get-tuple-element.73.refs_3_, ...), custom_call_target="tpu_custom_call" | custom-call | tf_op jit(solution)/shard_map/attend/pallas_call | solution.py:205
  117.8 5.9 %term.1 = bf16[32,48,512]{2,1,0:T(8,128)(2,1)} custom-call(bf16[32,256]{1,0:T(8,128)(2,1)S(1)} %get-tuple-element.74.mid, bf16[16,512]{1,0:T(8,128)(2,1)S(1)} %get-tuple-element.75.up_sum, bf16[256,16384]{1,0:T(8,128)(2,1)} %tok.1), custom_call_target="tpu_custom_call" | custom-call | tf_op jit(solution)/shard_map/term/pallas_call | solution.py:232
  123.8 5.2 %all-to-all-start = ((bf16[32,48,512]{2,1,0:T(8,128)(2,1)}), bf16[32,48,512]{2,1,0:T(8,128)(2,1)S(1)}, u32[]{:S(2)}, u32[]{:S(2)}) async-start(bf16[32,48,512]{2,1,0:T(8,128)(2,1)} %term.1), calls=%async_computation | async-start | bytes 3145728 | tf_op jit(solution)/shard_map/all_to_all | solution.py:414
  129.0 14.8 %output.1 = bf16[256,16384]{1,0:T(8,128)(2,1)} custom-call(s32[5]{0:T(128)S(1)} %copy-done, bf16[256,256]{1,0:T(8,128)(2,1)S(1)} %get-tuple-element.76.context, bf16[16,256,256]{2,1,0:T(8,128)(2,1)} %get-tuple-element.77.own, bf16[16,256,256]{2,1,0:T(8,128)(2,1)} %get-tuple-element.78.flipped, bf16[16,256,256]{2,1,0:T(8,128)(2,1)} %collective-permute-done.18.their_own, ...), custom_call_target="tpu_custom_call" | custom-call | flops 2147483648 | bytes 16777216 | tf_op jit(solution)/shard_map/output/pallas_call | solution.py:275
  143.8 11.7 %all-to-all-done.got = bf16[32,48,512]{2,1,0:T(8,128)(2,1)S(1)} async-done(((bf16[32,48,512]{2,1,0:T(8,128)(2,1)}), bf16[32,48,512]{2,1,0:T(8,128)(2,1)S(1)}, u32[]{:S(2)}, u32[]{:S(2)}) %all-to-all-start) | async-done | bytes 1572896 | tf_op jit(solution)/shard_map/all_to_all | solution.py:414
  155.5 1.2 total.1
  (22 shorter events, 0.1 us)
Async XLA Ops:
  0.6 22.9 %collective-permute-start.4 = (bf16[256,16384]{1,0:T(8,128)(2,1)}, bf16[256,16384]{1,0:T(8,128)(2,1)}, u32[]{:S(2)}, u32[]{:S(2)}) collective-permute-start(bf16[256,16384]{1,0:T(8,128)(2,1)} %tok.1), channel_id=1, source_target_pairs={{0,1},{1,0},{2,3},{3,2},{4,5},{5,4},{6,7},{7,6},{8,9},{9,8},{10,11... | collective-permute-start | bytes 25165832 | tf_op jit(solution)/shard_map/ppermute | solution.py:356
  4.6 15.3 %collective-permute-start.3 = (bf16[896,256]{1,0:T(8,128)(2,1)}, bf16[896,256]{1,0:T(8,128)(2,1)S(1)}, u32[]{:S(2)}, u32[]{:S(2)}) collective-permute-start(bf16[896,256]{1,0:T(8,128)(2,1)} %pack.1), channel_id=1, source_target_pairs={{0,24},{1,97},{2,26},{3,99},{4,28},{5,101},{6,30},{7,103},{8,0},{9... | collective-permute-start | bytes 1376264 | tf_op jit(solution)/shard_map/ppermute | solution.py:353
  8.7 11.2 %collective-permute-start.2 = (bf16[896,256]{1,0:T(8,128)(2,1)}, bf16[896,256]{1,0:T(8,128)(2,1)S(1)}, u32[]{:S(2)}, u32[]{:S(2)}) collective-permute-start(bf16[896,256]{1,0:T(8,128)(2,1)} %pack.1), channel_id=1, source_target_pairs={{0,16},{1,65},{2,18},{3,67},{4,20},{5,69},{6,22},{7,71},{8,24},{9,... | collective-permute-start | bytes 1376264 | tf_op jit(solution)/shard_map/ppermute | solution.py:353
  8.7 14.8 %collective-permute-start.1 = (bf16[896,256]{1,0:T(8,128)(2,1)}, bf16[896,256]{1,0:T(8,128)(2,1)S(1)}, u32[]{:S(2)}, u32[]{:S(2)}) collective-permute-start(bf16[896,256]{1,0:T(8,128)(2,1)} %pack.1), channel_id=1, source_target_pairs={{0,8},{1,33},{2,10},{3,35},{4,12},{5,37},{6,14},{7,39},{8,16},{9,4... | collective-permute-start | bytes 1376264 | tf_op jit(solution)/shard_map/ppermute | solution.py:353
  9.9 13.6 %collective-permute-start = (bf16[896,256]{1,0:T(8,128)(2,1)}, bf16[896,256]{1,0:T(8,128)(2,1)S(1)}, u32[]{:S(2)}, u32[]{:S(2)}) collective-permute-start(bf16[896,256]{1,0:T(8,128)(2,1)} %pack.1), channel_id=1, source_target_pairs={{0,4},{4,0},{8,12},{12,8},{16,20},{20,16},{24,28},{28,24},{32,36},... | collective-permute-start | bytes 1376264 | tf_op jit(solution)/shard_map/ppermute | solution.py:361
  24.8 33.7 %collective-permute-start.9 = (bf16[4,896,256]{2,1,0:T(8,128)(2,1)S(1)}, bf16[4,896,256]{2,1,0:T(8,128)(2,1)S(1)}, u32[]{:S(2)}, u32[]{:S(2)}) collective-permute-start(bf16[4,896,256]{2,1,0:T(8,128)(2,1)S(1)} %pad_maximum_fusion.refs_8_.refs_9_), channel_id=1, source_target_pairs={{0,96},{1,25},{2,98},{3,27},{4,100},{5,29},{6,102},{7,31},{8,104},... | collective-permute-start | bytes 5505032 | tf_op jit(solution)/shard_map/ppermute | solution.py:353
  27.8 34.3 %collective-permute-start.8 = (bf16[4,896,256]{2,1,0:T(8,128)(2,1)S(1)}, bf16[4,896,256]{2,1,0:T(8,128)(2,1)S(1)}, u32[]{:S(2)}, u32[]{:S(2)}) collective-permute-start(bf16[4,896,256]{2,1,0:T(8,128)(2,1)S(1)} %pad_maximum_fusion.refs_8_.refs_9_), channel_id=1, source_target_pairs={{0,32},{1,9},{2,34},{3,11},{4,36},{5,13},{6,38},{7,15},{8,40},{9,1... | collective-permute-start | bytes 5505032 | tf_op jit(solution)/shard_map/ppermute | solution.py:353
  27.9 14.6 %collective-permute-start.7 = (bf16[896,256]{1,0:T(8,128)(2,1)S(1)}, bf16[896,256]{1,0:T(8,128)(2,1)S(1)}, u32[]{:S(2)}, u32[]{:S(2)}) collective-permute-start(bf16[896,256]{1,0:T(8,128)(2,1)S(1)} %collective-permute-done), channel_id=1, source_target_pairs={{0,24},{1,97},{2,26},{3,99},{4,28},{5,101},{6,30},{7,103},{8,0},{9... | collective-permute-start | bytes 1376264 | tf_op jit(solution)/shard_map/ppermute | solution.py:353
  30.7 15.0 %collective-permute-start.6 = (bf16[896,256]{1,0:T(8,128)(2,1)S(1)}, bf16[896,256]{1,0:T(8,128)(2,1)S(1)}, u32[]{:S(2)}, u32[]{:S(2)}) collective-permute-start(bf16[896,256]{1,0:T(8,128)(2,1)S(1)} %collective-permute-done), channel_id=1, source_target_pairs={{0,16},{1,65},{2,18},{3,67},{4,20},{5,69},{6,22},{7,71},{8,24},{9,... | collective-permute-start | bytes 1376264 | tf_op jit(solution)/shard_map/ppermute | solution.py:353
  30.7 20.8 %collective-permute-start.5 = (bf16[896,256]{1,0:T(8,128)(2,1)S(1)}, bf16[896,256]{1,0:T(8,128)(2,1)S(1)}, u32[]{:S(2)}, u32[]{:S(2)}) collective-permute-start(bf16[896,256]{1,0:T(8,128)(2,1)S(1)} %collective-permute-done), channel_id=1, source_target_pairs={{0,8},{1,33},{2,10},{3,35},{4,12},{5,37},{6,14},{7,39},{8,16},{9,4... | collective-permute-start | bytes 1376264 | tf_op jit(solution)/shard_map/ppermute | solution.py:353
  58.4 6.1 %copy-start.1 = (bf16[4,896,256]{2,1,0:T(8,128)(2,1)}, bf16[4,896,256]{2,1,0:T(8,128)(2,1)S(1)}, u32[]{:S(2)}) copy-start(bf16[4,896,256]{2,1,0:T(8,128)(2,1)S(1)} %collective-permute-done.9.refs_12_.refs_13_) | copy-start | bytes 5505028
  62.1 13.5 %collective-permute-start.10 = (bf16[256,16384]{1,0:T(8,128)(2,1)}, bf16[256,16384]{1,0:T(8,128)(2,1)}, u32[]{:S(2)}, u32[]{:S(2)}) collective-permute-start(bf16[256,16384]{1,0:T(8,128)(2,1)} %refs_3_.9), channel_id=1, source_target_pairs={{0,1},{1,0},{2,3},{3,2},{4,5},{5,4},{6,7},{7,6},{8,9},{9,8},{10,11... | collective-permute-start | bytes 25165832 | tf_op jit(solution)/shard_map/ppermute | solution.py:356
  62.4 13.3 %copy-start = (s32[5]{0:T(128)S(1)}, s32[5]{0:T(128)}, u32[]{:S(2)}) copy-start(s32[5]{0:T(128)} %stack.53.where) | copy-start | bytes 64
  62.4 27.4 %collective-permute-start.12 = (bf16[4,896,256]{2,1,0:T(8,128)(2,1)S(1)}, bf16[4,896,256]{2,1,0:T(8,128)(2,1)S(1)}, u32[]{:S(2)}, u32[]{:S(2)}) collective-permute-start(bf16[4,896,256]{2,1,0:T(8,128)(2,1)S(1)} %pad_maximum_fusion.1.refs_8_.refs_9_), channel_id=1, source_target_pairs={{0,96},{1,25},{2,98},{3,27},{4,100},{5,29},{6,102},{7,31},{8,104},... | collective-permute-start | bytes 5505032 | tf_op jit(solution)/shard_map/ppermute | solution.py:353
  63.2 26.5 %collective-permute-start.11 = (bf16[4,896,256]{2,1,0:T(8,128)(2,1)S(1)}, bf16[4,896,256]{2,1,0:T(8,128)(2,1)S(1)}, u32[]{:S(2)}, u32[]{:S(2)}) collective-permute-start(bf16[4,896,256]{2,1,0:T(8,128)(2,1)S(1)} %pad_maximum_fusion.1.refs_8_.refs_9_), channel_id=1, source_target_pairs={{0,32},{1,9},{2,34},{3,11},{4,36},{5,13},{6,38},{7,15},{8,40},{9,1... | collective-permute-start | bytes 5505032 | tf_op jit(solution)/shard_map/ppermute | solution.py:353
  64.6 35.3 %collective-permute-start.16 = (bf16[2,896,256]{2,1,0:T(8,128)(2,1)S(1)}, bf16[2,896,256]{2,1,0:T(8,128)(2,1)S(1)}, u32[]{:S(2)}, u32[]{:S(2)}) collective-permute-start(bf16[2,896,256]{2,1,0:T(8,128)(2,1)S(1)} %slice.18), channel_id=1, source_target_pairs={{0,96},{1,25},{2,98},{3,27},{4,100},{5,29},{6,102},{7,31},{8,104},... | collective-permute-start | bytes 2752520 | tf_op jit(solution)/shard_map/ppermute | solution.py:353
  66.7 33.2 %collective-permute-start.15 = (bf16[2,896,256]{2,1,0:T(8,128)(2,1)S(1)}, bf16[2,896,256]{2,1,0:T(8,128)(2,1)S(1)}, u32[]{:S(2)}, u32[]{:S(2)}) collective-permute-start(bf16[2,896,256]{2,1,0:T(8,128)(2,1)S(1)} %slice.17), channel_id=1, source_target_pairs={{0,32},{1,9},{2,34},{3,11},{4,36},{5,13},{6,38},{7,15},{8,40},{9,1... | collective-permute-start | bytes 2752520 | tf_op jit(solution)/shard_map/ppermute | solution.py:353
  89.9 17.4 %collective-permute-start.13 = (bf16[2,896,256]{2,1,0:T(8,128)(2,1)S(1)}, bf16[2,896,256]{2,1,0:T(8,128)(2,1)S(1)}, u32[]{:S(2)}, u32[]{:S(2)}) collective-permute-start(bf16[2,896,256]{2,1,0:T(8,128)(2,1)S(1)} %slice.15), channel_id=1, source_target_pairs={{0,32},{1,9},{2,34},{3,11},{4,36},{5,13},{6,38},{7,15},{8,40},{9,1... | collective-permute-start | bytes 2752520 | tf_op jit(solution)/shard_map/ppermute | solution.py:353
  90.1 17.3 %collective-permute-start.14 = (bf16[2,896,256]{2,1,0:T(8,128)(2,1)S(1)}, bf16[2,896,256]{2,1,0:T(8,128)(2,1)S(1)}, u32[]{:S(2)}, u32[]{:S(2)}) collective-permute-start(bf16[2,896,256]{2,1,0:T(8,128)(2,1)S(1)} %slice.16), channel_id=1, source_target_pairs={{0,96},{1,25},{2,98},{3,27},{4,100},{5,29},{6,102},{7,31},{8,104},... | collective-permute-start | bytes 2752520 | tf_op jit(solution)/shard_map/ppermute | solution.py:353
  107.3 8.8 %copy-start.2 = (bf16[2,16,384]{2,1,0:T(8,128)(2,1)S(1)}, bf16[2,16,384]{2,1,0:T(8,128)(2,1)}, u32[]{:S(2)}) copy-start(bf16[2,16,384]{2,1,0:T(8,128)(2,1)} %param.17) | copy-start | bytes 73732
  111.8 3.1 %collective-permute-start.17 = (f32[256,768]{1,0:T(8,128)S(1)}, f32[256,768]{1,0:T(8,128)S(1)}, u32[]{:S(2)}, u32[]{:S(2)}) collective-permute-start(f32[256,768]{1,0:T(8,128)S(1)} %slice.19), channel_id=1, source_target_pairs={{0,1},{1,0},{2,3},{3,2},{4,5},{5,4},{6,7},{7,6},{8,9},{9,8},{10,11... | collective-permute-start | bytes 2359304 | tf_op jit(solution)/shard_map/ppermute | solution.py:356
  114.8 14.2 %collective-permute-start.18 = (bf16[16,256,256]{2,1,0:T(8,128)(2,1)}, bf16[16,256,256]{2,1,0:T(8,128)(2,1)}, u32[]{:S(2)}, u32[]{:S(2)}) collective-permute-start(bf16[16,256,256]{2,1,0:T(8,128)(2,1)} %get-tuple-element.77.own), channel_id=1, source_target_pairs={{0,1},{1,0},{2,3},{3,2},{4,5},{5,4},{6,7},{7,6},{8,9},{9,8},{10,11... | collective-permute-start | bytes 6291464 | tf_op jit(solution)/shard_map/ppermute | solution.py:356
  115.2 13.8 %collective-permute-start.19 = (bf16[16,256,256]{2,1,0:T(8,128)(2,1)}, bf16[16,256,256]{2,1,0:T(8,128)(2,1)}, u32[]{:S(2)}, u32[]{:S(2)}) collective-permute-start(bf16[16,256,256]{2,1,0:T(8,128)(2,1)} %get-tuple-element.78.flipped), channel_id=1, source_target_pairs={{0,1},{1,0},{2,3},{3,2},{4,5},{5,4},{6,7},{7,6},{8,9},{9,8},{10,11... | collective-permute-start | bytes 6291464 | tf_op jit(solution)/shard_map/ppermute | solution.py:356
  123.8 31.7 %all-to-all-start = ((bf16[32,48,512]{2,1,0:T(8,128)(2,1)}), bf16[32,48,512]{2,1,0:T(8,128)(2,1)S(1)}, u32[]{:S(2)}, u32[]{:S(2)}) async-start(bf16[32,48,512]{2,1,0:T(8,128)(2,1)} %term.1), calls=%async_computation | async-start | bytes 3145728 | tf_op jit(solution)/shard_map/all_to_all | solution.py:414
